TPU v7x, 128 devices: a whole 4x4x4 slice. The times are simulated.
128 devices in a mesh: obj: 16 (over y, z), pat: 8 (over x, core).
Axes of the slice: x: 4, y: 4, z: 4, core: 2. Of those that a mesh axis runs over, the one named last changes fastest.
Arguments:
- object_field: float32 [2, 2048, 2048], P(None, 'obj', 'pat'), may hold values from -6 to 6
- probe: float32 [2, 512, 512], replicated, may hold values from -5 to 5
- scan_cols: int32 [256], P(('obj', 'pat')), may hold values from -1 to 24, as said below
- amplitudes: float32 [256, 512, 512], P(('obj', 'pat')), may hold values from 0.05 to 3
Outputs:
- object_next: float32 [2, 2048, 2048], P(None, 'obj', 'pat')
- probe_next: float32 [2, 512, 512], replicated
Inputs may be any that keep to these rules, and one draw needn't show every extreme that they name: `scan_cols`: the first slot of every worker is filled; within a band group the filled slots name distinct columns; every band group has a slot at column 24.
All inputs are finite; a program needn't handle non-finite values.
Results may differ from a plain program's by a relative error of at most 0.015.
Values sent between devices are 32-bit elements; how exact they have to be, the bound alone decides.
A program may use at most 128 MiB of HBM per device.

v0:
```python
import math

import jax
import jax.numpy as jnp
from jax import lax
from jax.sharding import PartitionSpec as P

ITERS = 2
SLOTS = 2


def passed_along(value, axis, steps):
    count = lax.axis_size(axis)
    leading, last = (max(0, -steps), min(count, count - steps))
    return lax.ppermute(value, axis, [(source, source + steps) for source in range(leading, last)])


def make_tables(size):
    index = jnp.arange(size, dtype=jnp.int32)
    product = index[:, None] * index[None, :] % size
    angle = product.astype(jnp.float32) * jnp.float32(2.0 * math.pi / size)
    scale = jnp.float32(1.0 / math.sqrt(size))
    real_part = jnp.cos(angle) * scale
    imag_part = -jnp.sin(angle) * scale
    fwd_left = jnp.concatenate(
        [jnp.concatenate([real_part, -imag_part], 1), jnp.concatenate([imag_part, real_part], 1)], 0
    )
    fwd_right = jnp.concatenate(
        [jnp.concatenate([real_part, imag_part], 1), jnp.concatenate([-imag_part, real_part], 1)], 0
    )
    return (fwd_left.astype(jnp.bfloat16), fwd_right.astype(jnp.bfloat16))


def transform(real_in, imag_in, left, right):
    size = real_in.shape[0]
    stacked = jnp.concatenate([real_in, imag_in], 0).astype(jnp.bfloat16)
    middle = jnp.dot(left, stacked, preferred_element_type=jnp.float32).astype(jnp.bfloat16)
    beside = jnp.concatenate([middle[:size], middle[size:]], 1)
    result = jnp.dot(beside, right, preferred_element_type=jnp.float32)
    return (result[:, :size], result[:, size:])


def exit_update(patch, probe, amplitude, valid, fwd_left, fwd_right):
    probe_re, probe_im = (probe[0], probe[1])
    patch_re, patch_im = (patch[0], patch[1])
    psi_re = probe_re * patch_re - probe_im * patch_im
    psi_im = probe_re * patch_im + probe_im * patch_re
    wave_re, wave_im = transform(psi_re, psi_im, fwd_left, fwd_right)
    magnitude = jnp.sqrt(wave_re * wave_re + wave_im * wave_im)
    factor = amplitude / jnp.maximum(magnitude, 0.25)
    back_re, back_im = transform(wave_re * factor, wave_im * factor, fwd_right, fwd_left)
    diff_re = (back_re - psi_re) * valid
    diff_im = (back_im - psi_im) * valid
    object_part = jnp.stack(
        [probe_re * diff_re + probe_im * diff_im, probe_re * diff_im - probe_im * diff_re]
    )
    probe_part = jnp.stack(
        [patch_re * diff_re + patch_im * diff_im, patch_re * diff_im - patch_im * diff_re]
    )
    return (object_part, probe_part)


def fetch_band(tile):
    pieces = [tile]
    for below in (1, 2, 3):
        pieces.append(passed_along(tile, "obj", -below))
    stacked = jnp.concatenate(pieces, 1)
    return lax.all_gather(stacked, "pat", axis=2, tiled=True)


def return_grad(band_grad, rows):
    summed = lax.psum_scatter(band_grad, "pat", scatter_dimension=2, tiled=True)
    tile_grad = summed[:, :rows]
    for above in (1, 2, 3):
        tile_grad = tile_grad + passed_along(
            summed[:, above * rows : (above + 1) * rows], "obj", above
        )
    return tile_grad


def body(object_field, probe, scan_cols, amplitudes):
    size = probe.shape[1]
    rows = object_field.shape[1]
    eighth = size // 8
    fwd_left, fwd_right = make_tables(size)
    valid_all = (scan_cols >= 0).astype(jnp.float32)
    local_count = jnp.sum(valid_all)
    for step in range(ITERS):
        band = fetch_band(object_field)
        band_grad = jnp.zeros(band.shape, jnp.float32)
        probe_grad = jnp.zeros(probe.shape, jnp.float32)
        for slot in range(SLOTS):
            col_start = jnp.maximum(scan_cols[slot], 0) * eighth
            patch = lax.dynamic_slice_in_dim(band, col_start, size, 2)
            object_part, probe_part = exit_update(
                patch, probe, amplitudes[slot], valid_all[slot], fwd_left, fwd_right
            )
            region = lax.dynamic_slice_in_dim(band_grad, col_start, size, 2)
            band_grad = lax.dynamic_update_slice_in_dim(
                band_grad, region + object_part, col_start, 2
            )
            probe_grad = probe_grad + probe_part
        probe_total, count_total = lax.psum((probe_grad, local_count), ("obj", "pat"))
        tile_grad = return_grad(band_grad, rows)
        object_field = object_field + 0.25 * tile_grad
        probe = probe + probe_total / count_total
    return (object_field, probe)


def solution(mesh):
    in_specs = (P(None, "obj", "pat"), P(), P(("obj", "pat")), P(("obj", "pat"), None, None))
    out_specs = (P(None, "obj", "pat"), P())
    return jax.shard_map(body, mesh=mesh, in_specs=in_specs, out_specs=out_specs, check_vma=False)
```

profile of v0, /device:TPU:1, one launch (start us, length us, event | category | flops | bytes accessed | tf_op | source)
XLA Modules:
  0.0 693.3 jit_solution(17604109723487489797)
XLA Ops:
  7.2 1.4 collective-permute-start.2
  8.7 1.3 collective-permute-start.1
  10.0 1.3 collective-permute-start
  11.3 9.9 %collective-permute-done.2 = f32[2,128,256]{2,1,0:T(8,128)S(1)} collective-permute-done((f32[2,128,256]{2,1,0:T(8,128)}, f32[2,128,256]{2,1,0:T(8,128)S(1)}, u32[]{:S(2)}, u32[]{:S(2)}) %collective-permute-start.2) | collective-permute-done | bytes 262176 | tf_op jit(solution)/shard_map/ppermute | solution.py:15
  21.1 5.7 collective-permute-done.1
  26.9 2.0 pad_maximum_fusion.6
  31.4 4.0 multiply_convert_fusion.8
  35.4 5.2 negate_convert_fusion
  40.6 45.1 %all-gather.3.cloned.1.call-done = f32[2,512,2048]{2,1,0:T(8,128)} async-done(((f32[2,512,256]{2,1,0:T(8,128)}), f32[2,512,2048]{2,1,0:T(8,128)}) %all-gather.3.cloned.1.call-update) | async-done | bytes 8388624 | tf_op jit(solution)/shard_map/all_gather | solution.py:68
  85.6 3.8 fusion.138
  89.5 1.3 convolution_convert_fusion.5
  90.9 1.3 convolution_convert_fusion.7
  92.3 1.3 fusion.30
  93.5 1.3 fusion.16
  96.2 1.3 convolution_convert_fusion.4
  97.6 1.3 convolution_convert_fusion.6
  99.0 1.3 fusion.37
  102.7 1.7 add_bitcast_fusion.4
  104.5 4.0 add_bitcast_fusion.5
  108.5 3.1 fusion.72
  111.7 4.4 broadcast.21.clone
  116.1 10.1 %dynamic_update_slice.12 = f32[2,512,2048]{2,1,0:T(8,128)} dynamic-update-slice(f32[2,512,2048]{2,1,0:T(8,128)} %broadcast.21.clone, f32[2,512,512]{2,1,0:T(8,128)S(1)} %pad_maximum_fusion.4, s32[]{:T(128)} %constant.13.clone.1, s32[]{:T(128)} %constant.13.clone.1, s32[]{:T(128)S(6)} %select_n.36) | dynamic-update-slice | bytes 4194308 | tf_op jit(solution)/shard_map/dynamic_update_slice | solution.py:99
  126.2 3.0 maximum_add_fusion
  129.2 11.5 %dynamic_update_slice.13 = f32[2,512,2048]{2,1,0:T(8,128)} dynamic-update-slice(f32[2,512,2048]{2,1,0:T(8,128)} %dynamic_update_slice.12, f32[2,512,512]{2,1,0:T(8,128)S(1)} %maximum_add_fusion, s32[]{:T(128)} %constant.13.clone.1, s32[]{:T(128)} %constant.13.clone.1, s32[]{:T(128)S(6)} %select_n.37) | dynamic-update-slice | bytes 4194308 | tf_op jit(solution)/shard_map/dynamic_update_slice | solution.py:99
  142.2 3.0 maximum_add_fusion.1
  145.3 48.1 %reduce-scatter.3.cloned.1.call-done = f32[2,512,256]{2,1,0:T(8,128)} async-done(((f32[2,512,2048]{2,1,0:T(8,128)}), f32[2,512,256]{2,1,0:T(8,128)}) %reduce-scatter.3.cloned.1.call-update) | async-done | bytes 1048592 | tf_op jit(solution)/shard_map/reduce_scatter | solution.py:72
  194.6 3.2 collective-permute-start.3
  197.8 4.2 collective-permute-start.5
  202.0 3.6 collective-permute-start.4
  206.1 4.3 collective-permute-done.4
  211.4 1.3 collective-permute-start.8
  212.7 1.3 collective-permute-start.7
  214.0 1.3 collective-permute-start.6
  215.3 13.7 %collective-permute-done.8 = f32[2,128,256]{2,1,0:T(8,128)S(1)} collective-permute-done((f32[2,128,256]{2,1,0:T(8,128)S(1)}, f32[2,128,256]{2,1,0:T(8,128)S(1)}, u32[]{:S(2)}, u32[]{:S(2)}) %collective-permute-start.8) | collective-permute-done | bytes 262176 | tf_op jit(solution)/shard_map/ppermute | solution.py:15
  231.6 77.5 %psum.25 = f32[]{:T(128)} all-reduce(f32[]{:T(128)} %fusion.109), channel_id=1, replica_groups=mesh['obj'=16,'pat'=8] {'obj','pat'}, use_global_device_ids=true, to_apply=%region_3.4 | all-reduce | flops 1 | bytes 8 | tf_op jit(solution)/shard_map/psum | solution.py:103
  309.1 51.4 %all-reduce.3.cloned.1.call-done = f32[2,512,512]{2,1,0:T(8,128)} async-done(((f32[2,512,512]{2,1,0:T(8,128)}), f32[2,512,512]{2,1,0:T(8,128)}) %all-reduce.3.cloned.1.call-update) | async-done | bytes 2097168 | tf_op jit(solution)/shard_map/psum | solution.py:103
  360.5 3.3 divide_add_fusion.1
  363.7 46.7 %all-gather.5.cloned.1.call-done = f32[2,512,2048]{2,1,0:T(8,128)} async-done(((f32[2,512,256]{2,1,0:T(8,128)}), f32[2,512,2048]{2,1,0:T(8,128)}) %all-gather.5.cloned.1.call-update) | async-done | bytes 8388624 | tf_op jit(solution)/shard_map/all_gather | solution.py:68
  410.4 3.9 fusion.130
  414.4 1.3 convolution_convert_fusion.1
  415.8 1.3 convolution_convert_fusion.3
  417.2 1.3 fusion.58
  418.5 1.3 fusion.44
  421.2 1.3 convolution_convert_fusion
  422.6 1.3 convolution_convert_fusion.2
  424.0 1.3 fusion.65
  425.3 1.3 fusion.51
  427.7 1.7 add_bitcast_fusion
  429.4 4.1 add_bitcast_fusion.1
  433.5 3.1 add_bitcast_fusion.3
  436.7 1.5 pad_maximum_fusion.5
  438.1 4.4 broadcast.21
  442.5 10.7 %dynamic_update_slice.14 = f32[2,512,2048]{2,1,0:T(8,128)} dynamic-update-slice(f32[2,512,2048]{2,1,0:T(8,128)} %broadcast.21, f32[2,512,512]{2,1,0:T(8,128)} %pad_maximum_fusion.5, s32[]{:T(128)} %constant.13.clone.1, s32[]{:T(128)} %constant.13.clone.1, s32[]{:T(128)S(6)} %select_n.36) | dynamic-update-slice | bytes 4194308 | tf_op jit(solution)/shard_map/dynamic_update_slice | solution.py:99
  453.2 4.3 maximum_add_fusion.2
  457.5 12.1 %dynamic_update_slice.15 = f32[2,512,2048]{2,1,0:T(8,128)} dynamic-update-slice(f32[2,512,2048]{2,1,0:T(8,128)} %dynamic_update_slice.14, f32[2,512,512]{2,1,0:T(8,128)} %maximum_add_fusion.2, s32[]{:T(128)} %constant.13.clone.1, s32[]{:T(128)} %constant.13.clone.1, s32[]{:T(128)S(6)} %select_n.37) | dynamic-update-slice | bytes 4194308 | tf_op jit(solution)/shard_map/dynamic_update_slice | solution.py:99
  469.7 3.7 maximum_add_fusion.3
  473.4 48.9 %reduce-scatter.5.cloned.1.call-done = f32[2,512,256]{2,1,0:T(8,128)} async-done(((f32[2,512,2048]{2,1,0:T(8,128)}), f32[2,512,256]{2,1,0:T(8,128)}) %reduce-scatter.5.cloned.1.call-update) | async-done | bytes 1048592 | tf_op jit(solution)/shard_map/reduce_scatter | solution.py:72
  522.3 1.9 fusion.146
  524.1 3.2 collective-permute-start.9
  527.3 4.2 collective-permute-start.11
  531.6 4.3 collective-permute-start.10
  535.9 144.5 %all-reduce.5.cloned.1.call-done = f32[2,512,512]{2,1,0:T(8,128)} async-done(((f32[2,512,512]{2,1,0:T(8,128)}), f32[2,512,512]{2,1,0:T(8,128)}) %all-reduce.5.cloned.1.call-update) | async-done | bytes 2097168 | tf_op jit(solution)/shard_map/psum | solution.py:103
  680.3 4.0 divide_add_fusion
  684.3 1.8 fusion.88
  (75 shorter events, 15.4 us)
Async XLA Ops:
  7.2 21.8 %copy-start.12 = (s32[2]{0:T(128)S(1)}, s32[2]{0:T(128)}, u32[]{:S(2)}) copy-start(s32[2]{0:T(128)} %param.6) | copy-start | bytes 28
  7.2 78.5 %copy-start = (f32[2,512,512]{2,1,0:T(8,128)S(1)}, f32[2,512,512]{2,1,0:T(8,128)}, u32[]{:S(2)}) copy-start(f32[2,512,512]{2,1,0:T(8,128)} %param.5) | copy-start | bytes 6291460
  7.2 78.5 %all-gather.3.cloned.1.call-start = ((), (), s32[]{:S(2)}) async-start(), calls=%async_computation.2 | async-start | bytes 9437184 | tf_op jit(solution)/shard_map/all_gather | solution.py:68
  7.2 13.9 %collective-permute-start.2 = (f32[2,128,256]{2,1,0:T(8,128)}, f32[2,128,256]{2,1,0:T(8,128)S(1)}, u32[]{:S(2)}, u32[]{:S(2)}) collective-permute-start(f32[2,128,256]{2,1,0:T(8,128)} %param.4), channel_id=1, source_target_pairs={{24,0},{32,8},{40,16},{48,24},{56,32},{64,40},{72,48},{80,56},{88,... | collective-permute-start | bytes 786440 | tf_op jit(solution)/shard_map/ppermute | solution.py:15
  8.7 18.2 %collective-permute-start.1 = (f32[2,128,256]{2,1,0:T(8,128)}, f32[2,128,256]{2,1,0:T(8,128)S(1)}, u32[]{:S(2)}, u32[]{:S(2)}) collective-permute-start(f32[2,128,256]{2,1,0:T(8,128)} %param.4), channel_id=1, source_target_pairs={{16,0},{24,8},{32,16},{40,24},{48,32},{56,40},{64,48},{72,56},{80,... | collective-permute-start | bytes 786440 | tf_op jit(solution)/shard_map/ppermute | solution.py:15
  10.0 16.9 %collective-permute-start = (f32[2,128,256]{2,1,0:T(8,128)}, f32[2,128,256]{2,1,0:T(8,128)S(1)}, u32[]{:S(2)}, u32[]{:S(2)}) collective-permute-start(f32[2,128,256]{2,1,0:T(8,128)} %param.4), channel_id=1, source_target_pairs={{8,0},{16,8},{24,16},{32,24},{40,32},{48,40},{56,48},{64,56},{72,6... | collective-permute-start | bytes 786440 | tf_op jit(solution)/shard_map/ppermute | solution.py:15
  28.9 164.5 %reduce-scatter.3.cloned.1.call-start = ((), (), s32[]{:S(2)}) async-start(), calls=%async_computation.3 | async-start | bytes 9437184 | tf_op jit(solution)/shard_map/reduce_scatter | solution.py:72
  35.4 64.9 %copy-start.6 = (bf16[512,512]{1,0:T(8,128)(2,1)}, bf16[512,512]{1,0:T(8,128)(2,1)S(1)}, u32[]{:S(2)}) copy-start(bf16[512,512]{1,0:T(8,128)(2,1)S(1)} %multiply_convert_fusion.8) | copy-start | bytes 1572868
  40.6 59.7 %copy-start.8 = (bf16[512,512]{1,0:T(8,128)(2,1)}, bf16[512,512]{1,0:T(8,128)(2,1)S(1)}, u32[]{:S(2)}) copy-start(bf16[512,512]{1,0:T(8,128)(2,1)S(1)} %get-tuple-element.96) | copy-start | bytes 1572868
  85.6 3.8 copy-start.10
  93.5 1.6 copy-start.1
  99.0 2.6 slice-start
  100.3 2.4 slice-start.1
  140.7 1.2 copy-start.3
  140.7 1.5 copy-start.4
  140.7 219.8 %all-reduce.3.cloned.1.call-start = ((), (), s32[]{:S(2)}) async-start(), calls=%async_computation.4 | async-start | bytes 4194304 | tf_op jit(solution)/shard_map/psum | solution.py:103
  145.2 65.1 %copy-start.5 = (f32[2,128,256]{2,1,0:T(8,128)S(1)}, f32[2,128,256]{2,1,0:T(8,128)}, u32[]{:S(2)}) copy-start(f32[2,128,256]{2,1,0:T(8,128)} %param.4) | copy-start | bytes 786436
  145.3 265.2 %all-gather.5.cloned.1.call-start = ((), (), s32[]{:S(2)}) async-start(), calls=%async_computation.5 | async-start | bytes 9437184 | tf_op jit(solution)/shard_map/all_gather | solution.py:68
  194.6 11.0 %collective-permute-start.3 = (f32[2,128,256]{2,1,0:T(8,128)S(1)}, f32[2,128,256]{2,1,0:T(8,128)S(1)}, u32[]{:S(2)}, u32[]{:S(2)}) collective-permute-start(f32[2,128,256]{2,1,0:T(8,128)S(1)} %get-tuple-element.81), channel_id=1, source_target_pairs={{0,8},{8,16},{16,24},{24,32},{32,40},{40,48},{48,56},{56,64},{64,7... | collective-permute-start | bytes 786440 | tf_op jit(solution)/shard_map/ppermute | solution.py:15
  197.8 8.3 %collective-permute-start.5 = (f32[2,128,256]{2,1,0:T(8,128)S(1)}, f32[2,128,256]{2,1,0:T(8,128)S(1)}, u32[]{:S(2)}, u32[]{:S(2)}) collective-permute-start(f32[2,128,256]{2,1,0:T(8,128)S(1)} %get-tuple-element.82), channel_id=1, source_target_pairs={{0,24},{8,32},{16,40},{24,48},{32,56},{40,64},{48,72},{56,80},{64,... | collective-permute-start | bytes 786440 | tf_op jit(solution)/shard_map/ppermute | solution.py:15
  202.0 8.4 %collective-permute-start.4 = (f32[2,128,256]{2,1,0:T(8,128)S(1)}, f32[2,128,256]{2,1,0:T(8,128)S(1)}, u32[]{:S(2)}, u32[]{:S(2)}) collective-permute-start(f32[2,128,256]{2,1,0:T(8,128)S(1)} %get-tuple-element.83), channel_id=1, source_target_pairs={{0,16},{8,24},{16,32},{24,40},{32,48},{40,56},{48,64},{56,72},{64,... | collective-permute-start | bytes 786440 | tf_op jit(solution)/shard_map/ppermute | solution.py:15
  211.4 17.6 %collective-permute-start.8 = (f32[2,128,256]{2,1,0:T(8,128)S(1)}, f32[2,128,256]{2,1,0:T(8,128)S(1)}, u32[]{:S(2)}, u32[]{:S(2)}) collective-permute-start(f32[2,128,256]{2,1,0:T(8,128)S(1)} %fusion.92), channel_id=1, source_target_pairs={{24,0},{32,8},{40,16},{48,24},{56,32},{64,40},{72,48},{80,56},{88,... | collective-permute-start | bytes 786440 | tf_op jit(solution)/shard_map/ppermute | solution.py:15
  212.7 17.2 %collective-permute-start.7 = (f32[2,128,256]{2,1,0:T(8,128)S(1)}, f32[2,128,256]{2,1,0:T(8,128)S(1)}, u32[]{:S(2)}, u32[]{:S(2)}) collective-permute-start(f32[2,128,256]{2,1,0:T(8,128)S(1)} %fusion.92), channel_id=1, source_target_pairs={{16,0},{24,8},{32,16},{40,24},{48,32},{56,40},{64,48},{72,56},{80,... | collective-permute-start | bytes 786440 | tf_op jit(solution)/shard_map/ppermute | solution.py:15
  214.0 15.9 %collective-permute-start.6 = (f32[2,128,256]{2,1,0:T(8,128)S(1)}, f32[2,128,256]{2,1,0:T(8,128)S(1)}, u32[]{:S(2)}, u32[]{:S(2)}) collective-permute-start(f32[2,128,256]{2,1,0:T(8,128)S(1)} %fusion.92), channel_id=1, source_target_pairs={{8,0},{16,8},{24,16},{32,24},{40,32},{48,40},{56,48},{64,56},{72,6... | collective-permute-start | bytes 786440 | tf_op jit(solution)/shard_map/ppermute | solution.py:15
  231.0 291.3 %reduce-scatter.5.cloned.1.call-start = ((), (), s32[]{:S(2)}) async-start(), calls=%async_computation.6 | async-start | bytes 9437184 | tf_op jit(solution)/shard_map/reduce_scatter | solution.py:72
  410.4 3.9 copy-start.7
  410.4 3.9 copy-start.9
  410.4 3.9 copy-start.11
  418.5 1.6 copy-start.2
  424.0 2.6 slice-start.2
  425.2 2.4 slice-start.3
  469.6 210.7 %all-reduce.5.cloned.1.call-start = ((), (), s32[]{:S(2)}) async-start(), calls=%async_computation.7 | async-start | bytes 4194304 | tf_op jit(solution)/shard_map/psum | solution.py:103
  524.1 160.2 %collective-permute-start.9 = (f32[2,128,256]{2,1,0:T(8,128)}, f32[2,128,256]{2,1,0:T(8,128)S(1)}, u32[]{:S(2)}, u32[]{:S(2)}) collective-permute-start(f32[2,128,256]{2,1,0:T(8,128)} %get-tuple-element.70), channel_id=1, source_target_pairs={{0,8},{8,16},{16,24},{24,32},{32,40},{40,48},{48,56},{56,64},{64,7... | collective-permute-start | bytes 786440 | tf_op jit(solution)/shard_map/ppermute | solution.py:15
  527.3 157.0 %collective-permute-start.11 = (f32[2,128,256]{2,1,0:T(8,128)S(1)}, f32[2,128,256]{2,1,0:T(8,128)S(1)}, u32[]{:S(2)}, u32[]{:S(2)}) collective-permute-start(f32[2,128,256]{2,1,0:T(8,128)S(1)} %get-tuple-element.71), channel_id=1, source_target_pairs={{0,24},{8,32},{16,40},{24,48},{32,56},{40,64},{48,72},{56,80},{64,... | collective-permute-start | bytes 786440 | tf_op jit(solution)/shard_map/ppermute | solution.py:15
  531.6 152.8 %collective-permute-start.10 = (f32[2,128,256]{2,1,0:T(8,128)S(1)}, f32[2,128,256]{2,1,0:T(8,128)}, u32[]{:S(2)}, u32[]{:S(2)}) collective-permute-start(f32[2,128,256]{2,1,0:T(8,128)S(1)} %get-tuple-element.72), channel_id=1, source_target_pairs={{0,16},{8,24},{16,32},{24,40},{32,48},{40,56},{48,64},{56,72},{64,... | collective-permute-start | bytes 786440 | tf_op jit(solution)/shard_map/ppermute | solution.py:15
Sparse Core Ops, SparseCore 0:
  29.0 56.6 all-gather.2
  140.8 52.5 reduce-scatter.2
  198.8 161.5 all-reduce.2
  362.0 48.3 all-gather.4
  469.8 52.4 reduce-scatter.4
  527.5 152.7 all-reduce.4
where the time goes:
time: 698 us; the launch traced here: 693 us
  waiting for transfers between devices  420 us (60%)
  blocking collectives  77.5 us (11%)
  other arithmetic  66.2 us (9%)
  local copies, waits for them, and re-layouts  62.3 us (9%)
  starting transfers between devices  30.8 us (4%)
  matrix products  20.6 us (3%)
  between operations  16.1 us (2%)
    psum x2, waiting for transfers between devices, body(): lax.psum((probe_grad, local_count), ('obj', 'pat'))  196 us
    reduce_scatter x2, waiting for transfers between devices, return_grad(): summed = lax.psum_scatter(band_grad, 'pat', scatter_dimension=2, tiled=True)  97 us
    all_gather x2, waiting for transfers between devices, fetch_band(): return lax.all_gather(stacked, 'pat', axis=2, tiled=True)  91.8 us
    psum x1, blocking collectives, body(): lax.psum((probe_grad, local_count), ('obj', 'pat'))  77.5 us
    dynamic_update_slice x4, local copies, waits for them, and re-layouts, body(): lax.dynamic_update_slice_in_dim(band_grad, region + object_part, col_star...  44.4 us
    ppermute x12, waiting for transfers between devices, passed_along(): lax.ppermute(value, axis, [(source, source + steps) for source in range(l...  35 us
    ppermute x12, starting transfers between devices, passed_along(): lax.ppermute(value, axis, [(source, source + steps) for source in range(l...  30.6 us
    another operation x6, other arithmetic  19.1 us
  transfers between devices with their start and end apart: 18, of which 12 were waited for; matrix products, arithmetic and copies ran while one was open for 4% of the time, Pallas kernels for 0%

commit v1 on v0

v1 whole, which is shorter than its diff:
```python
import functools
import math

import jax
import jax.numpy as jnp
import ml_dtypes
import numpy as np
from jax import lax
from jax.experimental import pallas as pl
from jax.experimental.pallas import tpu as pltpu
from jax.sharding import PartitionSpec as P

N = 512
RB = 128
SLOTS = 2
TILES = 16
MESH = pl.DeviceIdType.MESH
F32 = jnp.float32
BF16 = jnp.bfloat16


def tables():
    index = np.arange(N)
    angle = (index[:, None] * index[None, :] % N) * (2.0 * math.pi / N)
    real = np.cos(angle) / math.sqrt(N)
    imag = -np.sin(angle) / math.sqrt(N)
    left = np.block([[real, -imag], [imag, real]])
    right = np.block([[real, imag], [-imag, real]])
    return left.astype(ml_dtypes.bfloat16), right.astype(ml_dtypes.bfloat16)


def place():
    o = lax.axis_index("obj")
    p = lax.axis_index("pat")
    return o // 4, lax.rem(o, 4), p // 2, lax.rem(p, 2)


def ring(value, step):
    return lax.rem(value + (step + 4), 4)


class Links:
    def __init__(self, send_sems, recv_sems):
        self.send_sems, self.recv_sems, self.used, self.copies = send_sems, recv_sems, 0, []
        self.y, self.z, self.x, self.c = place()

    def target(self, dy=0, dz=0, dx=0, dc=0):
        core = self.c if dc == 0 else 1 - self.c
        return (ring(self.y, dy) * 4 + ring(self.z, dz), ring(self.x, dx) * 2 + core)

    def send(self, src, dst, device):
        k = self.used
        self.used += 1
        copy = pltpu.make_async_remote_copy(
            src_ref=src, dst_ref=dst, send_sem=self.send_sems.at[k], recv_sem=self.recv_sems.at[k],
            device_id=device, device_id_type=MESH,
        )
        copy.start()
        self.copies.append(copy)
        return copy

    def group(self, step):
        o = lax.axis_index("obj")
        return (lax.rem(o + (step + 16), 16), lax.axis_index("pat"))

    def drain(self):
        for copy in self.copies:
            copy.wait_send()


def greet(devices):
    barrier = pltpu.get_barrier_semaphore()
    for device in devices:
        pl.semaphore_signal(barrier, inc=1, device_id=device, device_id_type=MESH)
    pl.semaphore_wait(barrier, len(devices))


def band_at(band, pat, b, half=None):
    if half is None:
        return band.at[pl.ds(2 * pat, 2), :, pl.ds(b * RB, RB), :]
    return band.at[pl.ds(2 * pat + half, 1), :, pl.ds(b * RB, RB), :]


def gather_steps(links, tile, band, local_sem):
    x, c = links.x, links.c
    me = 2 * x + c
    sib = links.target(dc=1)
    up, down = links.target(dx=1), links.target(dx=-1)
    before, after, across = 2 * ring(x, -1) + c, 2 * ring(x, 1) + c, 2 * ring(x, 2) + c
    state = {}

    def start():
        own = pltpu.make_async_copy(tile, band_at(band, me, 0), local_sem)
        own.start()
        state["own"] = own
        state["yz"] = {b: links.send(tile, band_at(band, me, b), links.group(-b)) for b in (1, 2, 3)}

    def first(b):
        src = tile
        if b:
            state["yz"][b].wait_recv()
            src = band_at(band, me, b)
        dst = band_at(band, me, b)
        state["up", b] = links.send(src, dst, up)
        state["down", b] = links.send(src, dst, down)
        state["sib", b] = [links.send(src, dst, sib)]

    def second(b):
        state["up", b].wait_recv()
        half, whole = band_at(band, before, b, 0), band_at(band, before, b)
        state["up2", b] = links.send(half, half, up)
        state["sib", b].append(links.send(whole, whole, sib))
        state["down", b].wait_recv()
        half, whole = band_at(band, after, b, 1), band_at(band, after, b)
        state["down2", b] = links.send(half, half, down)
        state["sib", b].append(links.send(whole, whole, sib))

    def third(b):
        state["up2", b].wait_recv()
        state["down2", b].wait_recv()
        whole = band_at(band, across, b)
        state["sib", b].append(links.send(whole, whole, sib))

    def finish():
        state["own"].wait()
        for b in range(4):
            for copy in state["sib", b]:
                copy.wait_recv()

    order = [start]
    for kind, b in ((first, 0), (first, 1), (second, 0), (first, 2), (second, 1), (third, 0), (first, 3),
                    (second, 2), (third, 1), (second, 3), (third, 2), (third, 3)):
        order.append(functools.partial(kind, b))
    return order + [finish]


GATHER_SENDS = 3 + 4 * 8


def gather_kernel(tile, band, send_sems, recv_sems, local_sem):
    links = Links(send_sems, recv_sems)
    groups = [links.group(s) for s in (-3, -2, -1, 1, 2, 3)]
    greet(groups + [links.target(dx=1), links.target(dx=-1), links.target(dc=1)])
    for step in gather_steps(links, tile, band, local_sem):
        step()
    links.drain()


def reduce_steps(links, grad, tile_in, tile_out, bufs, local_sems):
    own, sibs, halves, wholes, rows = bufs
    x, c = links.x, links.c
    o = lax.axis_index("obj")
    sib = links.target(dc=1)
    up, down = links.target(dx=1), links.target(dx=-1)
    before, after, across = ring(x, -1), ring(x, 1), ring(x, 2)
    state = {}

    def start():
        for b in (3, 2, 1, 0):
            mine = grad.at[:, c, :, :, pl.ds(b * RB, RB), :]
            theirs = grad.at[:, 1 - c, :, :, pl.ds(b * RB, RB), :]
            state["sib", b] = links.send(theirs, sibs.at[b], sib)
            copy = pltpu.make_async_copy(mine, own.at[b], local_sems.at[b])
            copy.start()
            state["own", b] = copy

    def first(b):
        state["own", b].wait()
        state["sib", b].wait_recv()

        @pl.loop(0, 4)
        def _(k):
            own[b, k] = own[b, k] + sibs[b, k]

        state["up", b] = links.send(own.at[b, across, 0], halves.at[b, 0], up)
        state["down", b] = links.send(own.at[b, across, 1], halves.at[b, 1], down)

    def second(b):
        state["up", b].wait_recv()
        own[b, after, 0] = own[b, after, 0] + halves[b, 0]
        state["up2", b] = links.send(own.at[b, after], wholes.at[b, 0], up)
        state["down", b].wait_recv()
        own[b, before, 1] = own[b, before, 1] + halves[b, 1]
        state["down2", b] = links.send(own.at[b, before], wholes.at[b, 1], down)

    def third(b):
        state["up2", b].wait_recv()
        state["down2", b].wait_recv()
        own[b, x] = own[b, x] + (wholes[b, 0] + wholes[b, 1])
        if b:
            state["rows", b] = links.send(own.at[b, x], rows.at[b - 1], links.group(b))

    def finish():
        total = own[0, x]
        for b in (1, 2, 3):
            state["rows", b].wait_recv()
            total = total + jnp.where(o >= b, rows[b - 1], 0.0)
        tile_out[...] = tile_in[...] + 0.25 * total

    order = [start]
    for kind, b in ((first, 3), (first, 2), (second, 3), (first, 1), (second, 2), (third, 3), (first, 0),
                    (second, 1), (third, 2), (second, 0), (third, 1), (third, 0)):
        order.append(functools.partial(kind, b))
    return order + [finish]


REDUCE_SENDS = 4 * 5 + 3


def probe_steps(links, part, probe, count_in, probe_out, bufs, local_sems):
    q, q_sib, q_y, sum_y, q_z, sum_z, q_x, fresh, counts, got = bufs
    y, z, x, c = links.y, links.z, links.x, links.c
    sib = links.target(dc=1)
    state = {}

    def pull(key, n):
        for copy in state.pop(key):
            copy.wait_recv()
        total = counts[n]
        for k in range(1 if n == 0 else 3):
            total = total + got[n, k]
        counts[n + 1] = total

    def start():
        state["s"] = [links.send(part.at[1 - c], q_sib, sib), links.send(count_in, got.at[0, 0], sib)]
        copy = pltpu.make_async_copy(part.at[c], q, local_sems.at[0])
        copy.start()
        state["q"] = copy
        counts[0] = count_in[...]

    def over_y():
        state["q"].wait()
        pull("s", 0)

        @pl.loop(0, 4)
        def _(k):
            rows = pl.ds(k * 128, 128)
            q[rows, :] = q[rows, :] + q_sib[rows, :]

        state["y"] = []
        for k in (1, 2, 3):
            dev = links.target(dy=k)
            state["y"].append(links.send(q.at[pl.ds(128 * ring(y, k), 128), :], q_y.at[k - 1], dev))
            state["y"].append(links.send(counts.at[1], got.at[1, k - 1], dev))

    def over_z():
        pull("y", 1)
        sum_y[...] = q[pl.ds(128 * y, 128), :] + q_y[0] + q_y[1] + q_y[2]
        state["z"] = []
        for k in (1, 2, 3):
            dev = links.target(dz=k)
            state["z"].append(links.send(sum_y.at[pl.ds(32 * ring(z, k), 32), :], q_z.at[k - 1], dev))
            state["z"].append(links.send(counts.at[2], got.at[2, k - 1], dev))

    def over_x():
        pull("z", 2)
        sum_z[...] = sum_y[pl.ds(32 * z, 32), :] + q_z[0] + q_z[1] + q_z[2]
        state["x"] = []
        for k in (1, 2, 3):
            dev = links.target(dx=k)
            state["x"].append(links.send(sum_z.at[pl.ds(8 * ring(x, k), 8), :], q_x.at[k - 1], dev))
            state["x"].append(links.send(counts.at[3], got.at[3, k - 1], dev))

    def back_x():
        pull("x", 3)
        row = 128 * y + 32 * z + 8 * x
        total = sum_z[pl.ds(8 * x, 8), :] + q_x[0] + q_x[1] + q_x[2]
        count = counts[4][:, :1]
        fresh[...] = probe[c, pl.ds(row, 8), :] + total / count
        spot = probe_out.at[c, pl.ds(row, 8), :]
        copy = pltpu.make_async_copy(fresh, spot, local_sems.at[1])
        copy.start()
        state["fresh"] = copy
        state["bx"] = [links.send(fresh, spot, links.target(dx=k)) for k in (1, 2, 3)]

    def back_z():
        state["fresh"].wait()
        for copy in state.pop("bx"):
            copy.wait_recv()
        spot = probe_out.at[c, pl.ds(128 * y + 32 * z, 32), :]
        state["bz"] = [links.send(spot, spot, links.target(dz=k)) for k in (1, 2, 3)]

    def back_y():
        for copy in state.pop("bz"):
            copy.wait_recv()
        spot = probe_out.at[c, pl.ds(128 * y, 128), :]
        state["by"] = [links.send(spot, spot, links.target(dy=k)) for k in (1, 2, 3)]

    def back_sib():
        for copy in state.pop("by"):
            copy.wait_recv()
        spot = probe_out.at[c]
        state["bs"] = links.send(spot, spot, sib)

    def finish():
        state["bs"].wait_recv()

    return [start, over_y, over_z, over_x, back_x, back_z, back_y, back_sib, finish]


PROBE_SENDS = 2 + 18 + 9 + 1


def step_kernel(gather, grad, part, tile_in, probe, count_in, *refs):
    refs = list(refs)
    tile_out, probe_out = refs[:2]
    refs = refs[2:]
    band = refs.pop(0) if gather else None
    reduce_bufs, refs = refs[:5], refs[5:]
    probe_bufs, refs = refs[:10], refs[10:]
    send_sems, recv_sems, local_sems = refs
    links = Links(send_sems, recv_sems)
    groups = [links.group(s) for s in (-3, -2, -1, 1, 2, 3)]
    far = [links.target(dy=k) for k in (1, 2, 3)] + [links.target(dz=k) for k in (1, 2, 3)]
    near = [links.target(dx=k) for k in (1, 2, 3)] + [links.target(dc=1)]
    greet(groups + far + near)
    reduce = reduce_steps(links, grad, tile_in, tile_out, reduce_bufs, local_sems)
    probes = probe_steps(links, part, probe, count_in, probe_out, probe_bufs, local_sems.at[pl.ds(4, 2)])
    order = reduce[:1] + probes[:1] + reduce[1:3] + probes[1:2] + reduce[3:6] + probes[2:3] + reduce[6:8] + probes[3:4]
    order += reduce[8:10] + probes[4:5] + reduce[10:11] + probes[5:6] + reduce[11:12] + probes[6:7] + reduce[12:]
    if gather:
        more = gather_steps(links, tile_out, band, local_sems.at[6])
        order += more[:6] + probes[7:8] + more[6:] + probes[8:]
    else:
        order += probes[7:]
    for step in order:
        step()
    links.drain()


def compute_kernel(cols, band, probe, amps, left, right, grad, probe_grad,
                   win, patch, prb, amp, lt, rt, xs, ws, yr, yi, gsum, sems):
    o = lax.axis_index("obj")

    def window(s):
        first = jnp.minimum(jnp.maximum(cols[s], 0) // 2, 11)
        return pltpu.make_async_copy(band.at[pl.ds(first, 5)], win.at[s], sems.at[s])

    loads = [
        pltpu.make_async_copy(probe, prb, sems.at[2]),
        pltpu.make_async_copy(left, lt, sems.at[3]),
        pltpu.make_async_copy(right, rt, sems.at[4]),
        pltpu.make_async_copy(amps, amp, sems.at[5]),
    ]
    window(0).start()
    for load in loads:
        load.start()
    window(1).start()

    @pl.loop(0, TILES + 1)
    def _(t):
        gsum[t] = jnp.zeros((2, N, 128), F32)

    lane = lax.broadcasted_iota(jnp.int32, (32, 128), 1)

    def product(lhs, rhs):
        return jnp.dot(lhs, rhs, preferred_element_type=F32)

    def left_pass(table):
        for n in range(2):
            cut = slice(256 * n, 256 * n + 256)
            mid = product(table[...], xs[:, cut]).astype(BF16)
            ws[:, cut] = mid[:N]
            ws[:, 512 + 256 * n:768 + 256 * n] = mid[N:]

    def right_pass(table):
        for n in range(2):
            cut = slice(256 * n, 256 * n + 256)
            yr[:, cut] = product(ws[...], table[:, cut])
            yi[:, cut] = product(ws[...], table[:, 512 + 256 * n:768 + 256 * n])

    def slot(s, carry):
        col = cols[s]
        place_col = jnp.maximum(col, 0)
        valid = (col >= 0).astype(F32)
        first = jnp.minimum(place_col // 2, 11)
        shift = place_col // 2 - first
        odd = lax.rem(place_col, 2) == 1
        window(s).wait()

        @pl.when(s == 0)
        def _():
            loads[0].wait()

        @pl.loop(0, 16)
        def _(m):
            rows = pl.ds(pl.multiple_of(m * 32, 32), 32)
            inside = o * RB + m * 32 < TILES * RB
            for j in range(4):
                cut = slice(128 * j, 128 * j + 128)
                near, far = j + shift, jnp.minimum(j + shift + 1, 4)
                value = []
                for part in range(2):
                    a, b = win[s, near, part, rows, :], win[s, far, part, rows, :]
                    moved = jnp.where(lane < 64, pltpu.roll(a, 64, 1), pltpu.roll(b, 64, 1))
                    v = jnp.where(inside, jnp.where(odd, moved, a), 0.0)
                    patch[part, rows, cut] = v
                    value.append(v)
                re, im = value
                pre, pim = prb[0, rows, cut], prb[1, rows, cut]
                xs[rows, cut] = (pre * re - pim * im).astype(BF16)
                xs[pl.ds(pl.multiple_of(512 + m * 32, 32), 32), cut] = (pre * im + pim * re).astype(BF16)

        @pl.when(s == 0)
        def _():
            loads[1].wait()
            loads[2].wait()

        left_pass(lt)
        right_pass(rt)

        @pl.when(s == 0)
        def _():
            loads[3].wait()

        @pl.loop(0, 16)
        def _(m):
            rows = pl.ds(pl.multiple_of(m * 32, 32), 32)
            re, im = yr[rows, :], yi[rows, :]
            factor = amp[s, rows, :] * lax.rsqrt(jnp.maximum(re * re + im * im, 0.0625))
            xs[rows, :] = (re * factor).astype(BF16)
            xs[pl.ds(pl.multiple_of(512 + m * 32, 32), 32), :] = (im * factor).astype(BF16)

        left_pass(rt)
        right_pass(lt)
        first_out = first + shift

        @pl.loop(0, 16)
        def _(m):
            rows = pl.ds(pl.multiple_of(m * 32, 32), 32)
            last = [jnp.zeros((32, 128), F32)] * 2
            for j in range(5):
                if j < 4:
                    cut = slice(128 * j, 128 * j + 128)
                    re, im = patch[0, rows, cut], patch[1, rows, cut]
                    pre, pim = prb[0, rows, cut], prb[1, rows, cut]
                    dre = (yr[rows, cut] - (pre * re - pim * im)) * valid
                    dim = (yi[rows, cut] - (pre * im + pim * re)) * valid
                    gre, gim = re * dre + im * dim, re * dim - im * dre
                    keep = s == 0
                    probe_grad[0, rows, cut] = jnp.where(keep, gre, probe_grad[0, rows, cut] + gre)
                    probe_grad[1, rows, cut] = jnp.where(keep, gim, probe_grad[1, rows, cut] + gim)
                    parts = [pre * dre + pim * dim, pre * dim - pim * dre]
                else:
                    parts = [jnp.zeros((32, 128), F32)] * 2
                for part in range(2):
                    turned = pltpu.roll(parts[part], 64, 1) if j < 4 else parts[part]
                    moved = jnp.where(lane < 64, last[part], turned)
                    last[part] = turned
                    t = first_out + j
                    gsum[t, part, rows, :] = gsum[t, part, rows, :] + jnp.where(odd, moved, parts[part])

        return carry

    lax.fori_loop(0, SLOTS, slot, 0)
    out = pltpu.make_async_copy(gsum.at[pl.ds(0, TILES)], grad, sems.at[6])
    out.start()
    out.wait()


ANY = pl.BlockSpec(memory_space=pl.ANY)
VMEM = pl.BlockSpec(memory_space=pltpu.VMEM)
SMEM = pl.BlockSpec(memory_space=pltpu.SMEM)
TILE = (2, 2, RB, 128)
BAND = (TILES, 2, N, 128)


def f32(*shape):
    return pltpu.VMEM(shape, F32)


def params(collective_id=None):
    if collective_id is None:
        return pltpu.CompilerParams(vmem_limit_bytes=56 << 20)
    return pltpu.CompilerParams(vmem_limit_bytes=56 << 20, collective_id=collective_id, has_side_effects=True)


def gather_call(tile):
    return pl.pallas_call(
        gather_kernel,
        name="gather_band",
        out_shape=jax.ShapeDtypeStruct(BAND, F32),
        in_specs=[VMEM],
        out_specs=ANY,
        scratch_shapes=[pltpu.SemaphoreType.DMA((GATHER_SENDS,))] * 2 + [pltpu.SemaphoreType.DMA],
        compiler_params=params(1),
    )(tile)


def compute_call(cols, band, probe, amplitudes, left, right):
    return pl.pallas_call(
        compute_kernel,
        name="slot_updates",
        out_shape=(jax.ShapeDtypeStruct(BAND, F32), jax.ShapeDtypeStruct((2, N, N), F32)),
        in_specs=[SMEM] + [ANY] * 5,
        out_specs=(ANY, VMEM),
        scratch_shapes=[
            f32(2, 5, 2, N, 128), f32(2, N, N), f32(2, N, N), f32(2, N, N),
            pltpu.VMEM((1024, 1024), BF16), pltpu.VMEM((1024, 1024), BF16),
            pltpu.VMEM((1024, N), BF16), pltpu.VMEM((N, 1024), BF16),
            f32(N, N), f32(N, N), f32(TILES + 1, 2, N, 128), pltpu.SemaphoreType.DMA((7,)),
        ],
        compiler_params=params(),
    )(cols, band, probe, amplitudes, left, right)


def step_call(gather, grad, part, tile, probe, count):
    shapes = [jax.ShapeDtypeStruct(TILE, F32), jax.ShapeDtypeStruct((2, N, N), F32)]
    specs = [VMEM, ANY]
    if gather:
        shapes.append(jax.ShapeDtypeStruct(BAND, F32))
        specs.append(ANY)
    sends = REDUCE_SENDS + PROBE_SENDS + (GATHER_SENDS if gather else 0)
    return pl.pallas_call(
        functools.partial(step_kernel, gather),
        name="sum_and_gather" if gather else "sum_only",
        out_shape=tuple(shapes),
        in_specs=[ANY, ANY, VMEM, VMEM, VMEM],
        out_specs=tuple(specs),
        scratch_shapes=[
            f32(4, 4, *TILE), f32(4, 4, *TILE), f32(4, 2, 2, RB, 128), f32(4, 2, *TILE), f32(3, *TILE),
            f32(N, N), f32(N, N), f32(3, 128, N), f32(128, N), f32(3, 32, N), f32(32, N), f32(3, 8, N), f32(8, N),
            f32(5, 8, 128), f32(4, 3, 8, 128),
            pltpu.SemaphoreType.DMA((sends,)), pltpu.SemaphoreType.DMA((sends,)), pltpu.SemaphoreType.DMA((7,)),
        ],
        compiler_params=params(2 if gather else 3),
    )(grad.reshape(4, 2, 2, 2, N, 128), part, tile, probe, count)


def body(object_field, probe, scan_cols, amplitudes):
    left, right = (jnp.asarray(t) for t in tables())
    tile = object_field.reshape(2, RB, 2, 128).transpose(2, 0, 1, 3)
    count = jnp.full((8, 128), jnp.sum((scan_cols >= 0).astype(F32)))
    band = gather_call(tile)
    grad, part = compute_call(scan_cols, band, probe, amplitudes, left, right)
    tile, probe, band = step_call(True, grad, part, tile, probe, count)
    grad, part = compute_call(scan_cols, band, probe, amplitudes, left, right)
    tile, probe = step_call(False, grad, part, tile, probe, count)
    return tile.transpose(1, 2, 0, 3).reshape(2, RB, 256), probe


def solution(mesh):
    in_specs = (P(None, "obj", "pat"), P(), P(("obj", "pat")), P(("obj", "pat"), None, None))
    out_specs = (P(None, "obj", "pat"), P())
    return jax.shard_map(body, mesh=mesh, in_specs=in_specs, out_specs=out_specs, check_vma=False)
```

time: 698 us -> 303 us (0.43)
  waiting for transfers between devices: 420 us -> 0 us
  Pallas kernels: 0 us -> 292 us
  blocking collectives: 77.5 us -> 0 us
  other arithmetic: 66.2 us -> 1.26 us
  local copies, waits for them, and re-layouts: 62.3 us -> 8.13 us
  starting transfers between devices: 30.8 us -> 0 us
  matrix products: 20.6 us -> 0 us
  between operations: 16.1 us -> 0.69 us
    pallas_call x0 -> x5, Pallas kernels: none -> 292 us  [the longest x2 184 us: step_call(): pl.pallas_call(functools.partial(step_kernel, gather), name='sum_and_gath...]
    psum x2 -> x0, waiting for transfers between devices: 196 us -> none  [body(): lax.psum((probe_grad, local_count), ('obj', 'pat'))]
    reduce_scatter x2 -> x0, waiting for transfers between devices: 97 us -> none  [return_grad(): summed = lax.psum_scatter(band_grad, 'pat', scatter_dimension=2, tiled=True)]
    all_gather x2 -> x0, waiting for transfers between devices: 91.8 us -> none  [fetch_band(): return lax.all_gather(stacked, 'pat', axis=2, tiled=True)]
    psum x1 -> x0, blocking collectives: 77.5 us -> none  [body(): lax.psum((probe_grad, local_count), ('obj', 'pat'))]
    dynamic_update_slice x4 -> x0, local copies, waits for them, and re-layouts: 44.4 us -> none  [body(): lax.dynamic_update_slice_in_dim(band_grad, region + object_part, col_star...]
    another operation x14 -> x0, other arithmetic: 38.5 us -> none
    ppermute x12 -> x0, waiting for transfers between devices: 35 us -> none  [passed_along(): lax.ppermute(value, axis, [(source, source + steps) for source in range(l...]
  transfers between devices with their start and end apart: 18 -> 0, of which waited for: 12 -> 0; matrix products, arithmetic and copies ran while one was open for 4% -> 0% of each run, Pallas kernels for 0% -> 0%
where the time goes in v1:
time: 303 us; the launch traced here: 302 us
  Pallas kernels  292 us (96%)
  local copies, waits for them, and re-layouts  8.13 us (3%)
    pallas_call x2, Pallas kernels, step_call(): pl.pallas_call(functools.partial(step_kernel, gather), name='sum_and_gath...  184 us
    pallas_call x1, Pallas kernels, gather_call(): pl.pallas_call(gather_kernel, name='gather_band', out_shape=jax.ShapeDtyp...  53.9 us
    pallas_call x2, Pallas kernels, compute_call(): pl.pallas_call(compute_kernel, name='slot_updates', out_shape=(jax.ShapeD...  53.7 us

profile of v1, /device:TPU:1, one launch (start us, length us, event | category | flops | bytes accessed | tf_op | source)
XLA Modules:
  0.0 302.2 jit_solution(17584239312270910811)
XLA Ops:
  0.6 1.3 fusion
  1.9 1.2 broadcast_in_dim.3.count_in
  3.1 1.1 copy.8
  4.2 0.8 copy.9
  5.0 53.9 %gather_band.1.band = f32[16,2,512,128]{3,2,1,0:T(8,128)} custom-call(f32[2,2,128,128]{3,2,1,0:T(8,128)} %bitcast.8), custom_call_target="tpu_custom_call" | custom-call | tf_op jit(solution)/shard_map/gather_band/pallas_call | solution.py:479
  59.0 26.9 %slot_updates.2 = (f32[16,2,512,128]{3,2,1,0:T(8,128)}, f32[2,512,512]{2,1,0:T(8,128)}) custom-call(s32[2]{0:T(128)} %cols.3, f32[16,2,512,128]{3,2,1,0:T(8,128)} %gather_band.1.band, f32[2,512,512]{2,1,0:T(8,128)} %probe.3, f32[2,512,512]{2,1,0:T(8,128)} %amps.3, bf16[1024,1024]{1,0:T(8,128)(2,1)} %constant.8.clone.left, bf16[1024,1024]{1,0:T(8,128)(2,1)} %constant.9.clone.right), custom_call_target="tpu_custom_call" | custom-call | tf_op jit(solution)/shard_map/slot_updates/pallas_call | solution.py:491
  85.8 97.6 %sum_and_gather.1 = (f32[2,2,128,128]{3,2,1,0:T(8,128)}, f32[2,512,512]{2,1,0:T(8,128)}, f32[16,2,512,128]{3,2,1,0:T(8,128)}) custom-call(f32[4,2,2,2,512,128]{5,4,3,2,1,0:T(8,128)} %bitcast.7, f32[2,512,512]{2,1,0:T(8,128)} %get-tuple-element.12.part, f32[2,2,128,128]{3,2,1,0:T(8,128)} %bitcast.9, f32[2,512,512]{2,1,0:T(8,128)} %probe.3, ...), custom_call_target="tpu_custom_call" | custom-call | tf_op jit(solution)/shard_map/sum_and_gather/pallas_call | solution.py:514
  183.4 26.9 %slot_updates.3 = (f32[16,2,512,128]{3,2,1,0:T(8,128)}, f32[2,512,512]{2,1,0:T(8,128)}) custom-call(s32[2]{0:T(128)} %cols.3, f32[16,2,512,128]{3,2,1,0:T(8,128)} %get-tuple-element.13.band, f32[2,512,512]{2,1,0:T(8,128)} %get-tuple-element.14.probe, f32[2,512,512]{2,1,0:T(8,128)} %amps.3, bf16[1024,1024]{1,0:T(8,128)(2,1)} %constant.8.clone.left, ...), custom_call_target="tpu_custom_call" | custom-call | tf_op jit(solution)/shard_map/slot_updates/pallas_call | solution.py:491
  210.3 86.9 %sum_only.1 = (f32[2,2,128,128]{3,2,1,0:T(8,128)}, f32[2,512,512]{2,1,0:T(8,128)}) custom-call(f32[4,2,2,2,512,128]{5,4,3,2,1,0:T(8,128)} %bitcast.6, f32[2,512,512]{2,1,0:T(8,128)} %get-tuple-element.16.part, f32[2,2,128,128]{3,2,1,0:T(8,128)} %get-tuple-element.17.tile_in, f32[2,512,512]{2,1,0:T(8,128)} %get-tuple-element.14.probe, ...), custom_call_target="tpu_custom_call" | custom-call | tf_op jit(solution)/shard_map/sum_only/pallas_call | solution.py:514
  297.2 1.1 copy.10
  298.3 0.8 copy.11
  299.1 3.1 %copy.13 = f32[2,512,512]{2,1,0:T(8,128)} copy(f32[2,512,512]{2,1,0:T(8,128)} %get-tuple-element.25) | data formatting | bytes 4194304

commit v2 on v0

v2 whole, which is shorter than its diff:
```python
import math

import jax
import jax.numpy as jnp
import ml_dtypes
import numpy as np
from jax import lax
from jax.experimental import pallas as pl
from jax.experimental.pallas import tpu as pltpu
from jax.sharding import PartitionSpec as P

N = 512
RB = 128
ITERS = 2
SLOTS = 2
GROUPS = 16
MESH = pl.DeviceIdType.MESH
F32 = jnp.float32
BF16 = jnp.bfloat16
TILE = (2, 2, RB, 128)
SENDS = 256


def tables():
    index = np.arange(N)
    angle = (index[:, None] * index[None, :] % N) * (2.0 * math.pi / N)
    real = np.cos(angle) / math.sqrt(N)
    imag = -np.sin(angle) / math.sqrt(N)
    left = np.block([[real, -imag], [imag, real]])
    right = np.block([[real, imag], [-imag, real]])
    return left.astype(ml_dtypes.bfloat16), right.astype(ml_dtypes.bfloat16)


def ring(value, step):
    return lax.rem(value + (step + 4), 4)


def rows_of(start, count):
    return pl.ds(pl.multiple_of(start, count), count)


class Links:
    def __init__(self, send_sems, recv_sems):
        self.send_sems, self.recv_sems, self.used, self.copies = send_sems, recv_sems, 0, []
        o, p = lax.axis_index("obj"), lax.axis_index("pat")
        self.o, self.p = o, p
        self.y, self.z, self.x, self.c = o // 4, lax.rem(o, 4), p // 2, lax.rem(p, 2)

    def target(self, dy=0, dz=0, dx=0, dc=0):
        core = self.c if dc == 0 else 1 - self.c
        return (ring(self.y, dy) * 4 + ring(self.z, dz), ring(self.x, dx) * 2 + core)

    def group(self, step):
        return (lax.rem(self.o + (step + GROUPS), GROUPS), self.p)

    def greet(self):
        near = [self.group(1), self.group(-1), self.target(dc=1)]
        for k in (1, 2, 3):
            near += [self.target(dy=k), self.target(dz=k), self.target(dx=k)]
        barrier = pltpu.get_barrier_semaphore()
        for device in near:
            pl.semaphore_signal(barrier, inc=1, device_id=device, device_id_type=MESH)
        pl.semaphore_wait(barrier, len(near))

    def send(self, src, dst, device):
        k = self.used
        self.used += 1
        copy = pltpu.make_async_remote_copy(
            src_ref=src, dst_ref=dst, send_sem=self.send_sems.at[k], recv_sem=self.recv_sems.at[k],
            device_id=device, device_id_type=MESH,
        )
        copy.start()
        self.copies.append(copy)
        return copy

    def drain(self):
        for copy in self.copies:
            copy.wait_send()
        self.copies = []


class Gather:
    def __init__(self, links, tile, bands):
        self.links, self.tile, self.bands = links, tile, bands
        x, c = links.x, links.c
        self.me = 2 * x + c
        self.sib, self.up, self.down = links.target(dc=1), links.target(dx=1), links.target(dx=-1)
        self.before, self.after, self.across = 2 * ring(x, -1) + c, 2 * ring(x, 1) + c, 2 * ring(x, 2) + c
        self.got = {}

    def at(self, b, pat, half=None):
        if half is None:
            return self.bands[b].at[pl.ds(2 * pat, 2)]
        return self.bands[b].at[pl.ds(2 * pat + half, 1)]

    def chain(self, b):
        src = self.tile if b == 0 else self.at(b, self.me)
        self.got["chain", b + 1] = self.links.send(src, self.at(b + 1, self.me), self.links.group(-1))

    def first(self, b):
        src = self.tile
        if b:
            self.got["chain", b].wait_recv()
            src = self.at(b, self.me)
        dst = self.at(b, self.me)
        self.got["up", b] = self.links.send(src, dst, self.up)
        self.got["down", b] = self.links.send(src, dst, self.down)
        if 0 < b < 3:
            self.chain(b)
        self.got["sib", b] = [self.links.send(src, dst, self.sib)]

    def second(self, b):
        for name, pat, half, onward in (("up", self.before, 0, self.up), ("down", self.after, 1, self.down)):
            self.got[name, b].wait_recv()
            part, whole = self.at(b, pat, half), self.at(b, pat)
            self.got[name + "2", b] = self.links.send(part, part, onward)
            self.got["sib", b].append(self.links.send(whole, whole, self.sib))

    def third(self, b):
        self.got["up2", b].wait_recv()
        self.got["down2", b].wait_recv()
        whole = self.at(b, self.across)
        self.got["sib", b].append(self.links.send(whole, whole, self.sib))

    def done(self, b):
        for copy in self.got["sib", b]:
            copy.wait_recv()


class Reduce:
    def __init__(self, links, own, theirs, sibs, halves, wholes, chained):
        self.links, self.own, self.theirs = links, own, theirs
        self.sibs, self.halves, self.wholes, self.chained = sibs, halves, wholes, chained
        self.sib, self.up, self.down = links.target(dc=1), links.target(dx=1), links.target(dx=-1)
        x = links.x
        self.before, self.after, self.across = ring(x, -1), ring(x, 1), ring(x, 2)
        self.got = {}

    def zeroth(self, b):
        self.got["sib", b] = self.links.send(self.theirs.at[b], self.sibs.at[b], self.sib)

    def first(self, b):
        own, sibs = self.own, self.sibs
        self.got["sib", b].wait_recv()

        @pl.loop(0, 4)
        def _(k):
            own[b, k] = own[b, k] + sibs[b, k]

        self.got["up", b] = self.links.send(own.at[b, self.across, 0], self.halves.at[b, 0], self.up)
        self.got["down", b] = self.links.send(own.at[b, self.across, 1], self.halves.at[b, 1], self.down)

    def second(self, b):
        own = self.own
        self.got["up", b].wait_recv()
        own[b, self.after, 0] = own[b, self.after, 0] + self.halves[b, 0]
        self.got["up2", b] = self.links.send(own.at[b, self.after], self.wholes.at[b, 0], self.up)
        self.got["down", b].wait_recv()
        own[b, self.before, 1] = own[b, self.before, 1] + self.halves[b, 1]
        self.got["down2", b] = self.links.send(own.at[b, self.before], self.wholes.at[b, 1], self.down)

    def third(self, b):
        own, x = self.own, self.links.x
        self.got["up2", b].wait_recv()
        self.got["down2", b].wait_recv()
        total = own[b, x] + (self.wholes[b, 0] + self.wholes[b, 1])
        if b < 3:
            self.got["chain", b].wait_recv()
            total = total + jnp.where(self.links.o > 0, self.chained[b], 0.0)
        if b:
            own[b, x] = total
            self.got["chain", b - 1] = self.links.send(own.at[b, x], self.chained.at[b - 1], self.links.group(1))
        return total


class ProbeSum:
    def __init__(self, links, grad, probe, bufs, counts, counted, need_count):
        self.links, self.grad, self.probe = links, grad, probe
        self.from_sib, self.r1, self.s1, self.r2, self.s2, self.r3 = bufs
        self.counts, self.counted, self.need = counts, counted, need_count
        self.sib = links.target(dc=1)
        self.got = []

    def pull(self):
        for copy in self.got:
            copy.wait_recv()
        self.got = []

    def put(self, src, dst, **step):
        self.got.append(self.links.send(src, dst, self.links.target(**step)))

    def count_out(self, n, axis):
        if self.need:
            for k in (1, 2, 3) if axis != "dc" else (1,):
                self.put(self.counts.at[n], self.counted.at[n, k - 1], **{axis: k})

    def count_in(self, n):
        if self.need:
            total = self.counts[n]
            for k in range(3 if n else 1):
                total = total + self.counted[n, k]
            self.counts[n + 1] = total

    def steps(self):
        links, grad, probe = self.links, self.grad, self.probe
        y, z, x, c = links.y, links.z, links.x, links.c
        lanes = (pl.ds(0, 256), pl.ds(256, 256))

        def start():
            self.put(grad.at[1 - c], self.from_sib, dc=1)
            self.count_out(0, "dc")

        def first():
            self.pull()
            self.count_in(0)

            @pl.loop(0, 8)
            def _(k):
                rows = rows_of(k * 64, 64)
                grad[c, rows, :] = grad[c, rows, :] + self.from_sib[rows, :]

            for k in (2, 1, 3):
                self.put(grad.at[c, rows_of(128 * ring(y, k), 128), lanes[0]], self.r1.at[0, k - 1], dy=k)
                self.put(grad.at[c, rows_of(128 * ring(z, k), 128), lanes[1]], self.r1.at[1, k - 1], dz=k)
            self.count_out(1, "dy")

        def second():
            self.pull()
            self.count_in(1)
            for h, place in ((0, y), (1, z)):
                total = grad[c, rows_of(128 * place, 128), lanes[h]]
                self.s1[h] = total + self.r1[h, 0] + self.r1[h, 1] + self.r1[h, 2]
            for k in (2, 1, 3):
                self.put(self.s1.at[0, rows_of(32 * ring(z, k), 32), :], self.r2.at[0, k - 1], dz=k)
                self.put(self.s1.at[1, rows_of(32 * ring(y, k), 32), :], self.r2.at[1, k - 1], dy=k)
            self.count_out(2, "dz")

        def third():
            self.pull()
            self.count_in(2)
            for h, place in ((0, z), (1, y)):
                total = self.s1[h, rows_of(32 * place, 32), :]
                self.s2[h] = total + self.r2[h, 0] + self.r2[h, 1] + self.r2[h, 2]
            for k in (2, 1, 3):
                self.put(self.s2.at[:, rows_of(8 * ring(x, k), 8), :], self.r3.at[k - 1], dx=k)
            self.count_out(3, "dx")

        def fourth():
            self.pull()
            self.count_in(3)
            total = self.s2[:, rows_of(8 * x, 8), :] + self.r3[0] + self.r3[1] + self.r3[2]
            count = self.counts[4][:, :1]
            for h, row in ((0, 128 * y + 32 * z + 8 * x), (1, 128 * z + 32 * y + 8 * x)):
                spot = rows_of(row, 8)
                probe[c, spot, lanes[h]] = probe[c, spot, lanes[h]] + total[h] / count
                for k in (2, 1, 3):
                    self.put(probe.at[c, spot, lanes[h]], probe.at[c, spot, lanes[h]], dx=k)

        def fifth():
            self.pull()
            for h, row, axis in ((0, 128 * y + 32 * z, "dz"), (1, 128 * z + 32 * y, "dy")):
                spot = probe.at[c, rows_of(row, 32), lanes[h]]
                for k in (2, 1, 3):
                    self.put(spot, spot, **{axis: k})

        def sixth():
            self.pull()
            for h, row, axis in ((0, 128 * y, "dy"), (1, 128 * z, "dz")):
                spot = probe.at[c, rows_of(row, 128), lanes[h]]
                for k in (2, 1, 3):
                    self.put(spot, spot, **{axis: k})

        def seventh():
            self.pull()
            self.put(probe.at[c], probe.at[c], dc=1)

        return [start, first, second, third, fourth, fifth, sixth, seventh, self.pull]


def kernel(cols, field, probe_in, amps, left, right, field_out, probe_out,
           band0, band1, band2, band3, tile, probe, amp, lt, rt, patch, flat, tall, wave, back, parts0, parts1,
           probe_grad, own, theirs, sibs, halves, wholes, chained,
           from_sib, r1, s1, r2, s2, r3, counts, counted, send_sems, recv_sems, sems):
    bands = (band0, band1, band2, band3)
    parts = (parts0, parts1)
    links = Links(send_sems, recv_sems)
    loads = [
        pltpu.make_async_copy(src, dst, sems.at[i])
        for i, (src, dst) in enumerate(((probe_in, probe), (left, lt), (right, rt), (amps, amp)))
    ]
    for load in loads:
        load.start()
    for t in range(2):
        tile[t] = field[:, :, 128 * t:128 * t + 128]
    for s in range(SLOTS):
        for edge in (0, 6):
            parts[s][edge] = jnp.zeros((2, RB, 128), F32)
    col = [jnp.maximum(cols[s], 0) for s in range(SLOTS)]
    base = [lax.div(col[s], 2) for s in range(SLOTS)]
    odd = [lax.rem(col[s], 2) == 1 for s in range(SLOTS)]
    valid = [(cols[s] >= 0).astype(F32) for s in range(SLOTS)]
    counts[0] = jnp.full((8, 128), valid[0] + valid[1], F32)
    lane = lax.broadcasted_iota(jnp.int32, (32, 128), 1)
    links.greet()

    def product(lhs, rhs):
        return jnp.dot(lhs, rhs, preferred_element_type=F32)

    def rows_in(b):
        inside = links.o + b < GROUPS
        for s in range(SLOTS):
            @pl.loop(0, 4)
            def _(m):
                rows = rows_of(m * 32, 32)
                whole = rows_of(b * RB + m * 32, 32)
                loaded = [[bands[b][jnp.minimum(base[s] + j, 15), part, rows, :] for j in range(5)] for part in (0, 1)]
                turned = [[pltpu.roll(v, 64, 1) for v in values] for values in loaded]
                for j in range(4):
                    cut = slice(128 * j, 128 * j + 128)
                    value = []
                    for part in range(2):
                        moved = jnp.where(lane < 64, turned[part][j], turned[part][j + 1])
                        v = jnp.where(inside, jnp.where(odd[s], moved, loaded[part][j]), 0.0)
                        patch[s, part, whole, cut] = v
                        value.append(v)
                    re, im = value
                    pre, pim = probe[0, whole, cut], probe[1, whole, cut]
                    flat[s, whole, cut] = (pre * re - pim * im).astype(BF16)
                    flat[s, whole, 512 + 128 * j:640 + 128 * j] = (pre * im + pim * re).astype(BF16)

            rows = slice(b * RB, b * RB + RB)
            mid = product(flat[s, rows, :], rt[...]).astype(BF16)
            tall[s, rows, :] = mid[:, :N]
            tall[s, N + b * RB:N + b * RB + RB, :] = mid[:, N:]

    def middle():
        for s in range(SLOTS):
            for n in range(2):
                cut = slice(256 * n, 256 * n + 256)
                wave[...] = product(lt[...], tall[s, :, cut])

                @pl.loop(0, 16)
                def _(m):
                    upper, lower = rows_of(m * 32, 32), rows_of(N + m * 32, 32)
                    re, im = wave[upper, :], wave[lower, :]
                    factor = amp[s, upper, cut] * lax.rsqrt(jnp.maximum(re * re + im * im, 0.0625))
                    tall[s, upper, cut] = (re * factor).astype(BF16)
                    tall[s, lower, cut] = (im * factor).astype(BF16)

                mid = product(rt[...], tall[s, :, cut]).astype(BF16)
                flat[s, :, cut] = mid[:N]
                flat[s, :, 512 + 256 * n:768 + 256 * n] = mid[N:]

    def rows_out(b):
        for s in range(SLOTS):
            back[...] = product(flat[s, b * RB:b * RB + RB, :], lt[...])

            @pl.loop(0, 4)
            def _(m):
                rows = rows_of(m * 32, 32)
                whole = rows_of(b * RB + m * 32, 32)
                last = [jnp.zeros((32, 128), F32)] * 2
                for j in range(5):
                    value = [jnp.zeros((32, 128), F32)] * 2
                    if j < 4:
                        cut = slice(128 * j, 128 * j + 128)
                        re, im = patch[s, 0, whole, cut], patch[s, 1, whole, cut]
                        pre, pim = probe[0, whole, cut], probe[1, whole, cut]
                        dre = (back[rows, cut] - (pre * re - pim * im)) * valid[s]
                        dim = (back[rows, 512 + 128 * j:640 + 128 * j] - (pre * im + pim * re)) * valid[s]
                        gre, gim = re * dre + im * dim, re * dim - im * dre
                        if s:
                            gre, gim = gre + probe_grad[0, whole, cut], gim + probe_grad[1, whole, cut]
                        probe_grad[0, whole, cut] = gre
                        probe_grad[1, whole, cut] = gim
                        value = [pre * dre + pim * dim, pre * dim - pim * dre]
                    for part in range(2):
                        turned = pltpu.roll(value[part], 64, 1) if j < 4 else value[part]
                        moved = jnp.where(lane < 64, last[part], turned)
                        last[part] = turned
                        parts[s][j + 1, part, rows, :] = jnp.where(odd[s], moved, value[part])

        def placed(t):
            spot = [jnp.clip(t - base[s], -1, 5) + 1 for s in range(SLOTS)]
            return parts[0][spot[0]] + parts[1][spot[1]]

        @pl.loop(0, 4)
        def _(k):
            for half in range(2):
                own[b, k, half] = placed(4 * k + 2 * links.c + half)
                theirs[b, k, half] = placed(4 * k + 2 * (1 - links.c) + half)

    for turn in range(ITERS):
        gather = Gather(links, tile, bands)
        gather.chain(0)
        gather.first(0)
        own_copy = pltpu.make_async_copy(tile, gather.at(0, gather.me), sems.at[4])
        own_copy.start()
        gather.second(0)
        gather.first(1)
        gather.third(0)
        if turn == 0:
            for load in loads:
                load.wait()
        else:
            tail[0]()
        own_copy.wait()
        gather.second(1)
        gather.first(2)
        if turn:
            tail[1]()
        gather.done(0)
        rows_in(0)
        gather.third(1)
        gather.second(2)
        gather.first(3)
        gather.done(1)
        rows_in(1)
        gather.third(2)
        gather.second(3)
        gather.done(2)
        rows_in(2)
        gather.third(3)
        gather.done(3)
        rows_in(3)
        links.drain()
        middle()
        reduce = Reduce(links, own, theirs, sibs, halves, wholes, chained)
        sums = ProbeSum(links, probe_grad, probe, (from_sib, r1, s1, r2, s2, r3), counts, counted, turn == 0).steps()
        rows_out(3)
        reduce.zeroth(3)
        rows_out(2)
        reduce.zeroth(2)
        reduce.first(3)
        rows_out(1)
        reduce.zeroth(1)
        reduce.first(2)
        reduce.second(3)
        rows_out(0)
        reduce.zeroth(0)
        sums[0]()
        reduce.first(1)
        sums[1]()
        reduce.second(2)
        reduce.third(3)
        reduce.first(0)
        sums[2]()
        reduce.second(1)
        sums[3]()
        reduce.third(2)
        sums[4]()
        reduce.second(0)
        sums[5]()
        reduce.third(1)
        sums[6]()
        total = reduce.third(0)
        tail = sums[7:]
        if turn < ITERS - 1:
            tile[...] = tile[...] + 0.25 * total
    for t in range(2):
        field_out[:, :, 128 * t:128 * t + 128] = tile[t] + 0.25 * total[t]
    tail[0]()
    mine = pltpu.make_async_copy(probe.at[links.c], probe_out.at[links.c], sems.at[5])
    mine.start()
    tail[1]()
    other = pltpu.make_async_copy(probe.at[1 - links.c], probe_out.at[1 - links.c], sems.at[6])
    other.start()
    links.drain()
    mine.wait()
    other.wait()


def f32(*shape):
    return pltpu.VMEM(shape, F32)


def body(object_field, probe, scan_cols, amplitudes):
    left, right = (jnp.asarray(t) for t in tables())
    anywhere = pl.BlockSpec(memory_space=pl.ANY)
    vmem = pl.BlockSpec(memory_space=pltpu.VMEM)
    return pl.pallas_call(
        kernel,
        name="reconstruct",
        out_shape=(jax.ShapeDtypeStruct((2, RB, 256), F32), jax.ShapeDtypeStruct((2, N, N), F32)),
        in_specs=[pl.BlockSpec(memory_space=pltpu.SMEM), vmem] + [anywhere] * 4,
        out_specs=(vmem, anywhere),
        scratch_shapes=[f32(16, 2, RB, 128)] * 4 + [
            f32(*TILE), f32(2, N, N), f32(2, N, N), pltpu.VMEM((1024, 1024), BF16), pltpu.VMEM((1024, 1024), BF16),
            f32(2, 2, N, N), pltpu.VMEM((2, N, 1024), BF16), pltpu.VMEM((2, 1024, N), BF16),
            f32(1024, 256), f32(RB, 1024), f32(7, 2, RB, 128), f32(7, 2, RB, 128),
            f32(2, N, N), f32(4, 4, *TILE), f32(4, 4, *TILE), f32(4, 4, *TILE),
            f32(4, 2, 2, RB, 128), f32(4, 2, *TILE), f32(3, *TILE),
            f32(N, N), f32(2, 3, 128, 256), f32(2, 128, 256), f32(2, 3, 32, 256), f32(2, 32, 256), f32(3, 2, 8, 256),
            f32(5, 8, 128), f32(4, 3, 8, 128),
            pltpu.SemaphoreType.DMA((SENDS,)), pltpu.SemaphoreType.DMA((SENDS,)), pltpu.SemaphoreType.DMA((7,)),
        ],
        compiler_params=pltpu.CompilerParams(vmem_limit_bytes=60 << 20, collective_id=1, has_side_effects=True),
    )(scan_cols, object_field, probe, amplitudes, left, right)


def solution(mesh):
    in_specs = (P(None, "obj", "pat"), P(), P(("obj", "pat")), P(("obj", "pat"), None, None))
    out_specs = (P(None, "obj", "pat"), P())
    return jax.shard_map(body, mesh=mesh, in_specs=in_specs, out_specs=out_specs, check_vma=False)
```

time: 698 us -> 235 us (0.34)
  waiting for transfers between devices: 420 us -> 0 us
  Pallas kernels: 0 us -> 230 us
  blocking collectives: 77.5 us -> 0 us
  other arithmetic: 66.2 us -> 0 us
  local copies, waits for them, and re-layouts: 62.3 us -> 4.75 us
  starting transfers between devices: 30.8 us -> 0 us
  matrix products: 20.6 us -> 0 us
  between operations: 16.1 us -> 0.64 us
    pallas_call x0 -> x1, Pallas kernels: none -> 230 us  [body(): pl.pallas_call(kernel, name='reconstruct', out_shape=(jax.ShapeDtypeStruc...]
    psum x2 -> x0, waiting for transfers between devices: 196 us -> none  [body(): lax.psum((probe_grad, local_count), ('obj', 'pat'))]
    reduce_scatter x2 -> x0, waiting for transfers between devices: 97 us -> none  [return_grad(): summed = lax.psum_scatter(band_grad, 'pat', scatter_dimension=2, tiled=True)]
    all_gather x2 -> x0, waiting for transfers between devices: 91.8 us -> none  [fetch_band(): return lax.all_gather(stacked, 'pat', axis=2, tiled=True)]
    psum x1 -> x0, blocking collectives: 77.5 us -> none  [body(): lax.psum((probe_grad, local_count), ('obj', 'pat'))]
    dynamic_update_slice x4 -> x0, local copies, waits for them, and re-layouts: 44.4 us -> none  [body(): lax.dynamic_update_slice_in_dim(band_grad, region + object_part, col_star...]
    another operation x14 -> x0, other arithmetic: 38.5 us -> none
    ppermute x12 -> x0, waiting for transfers between devices: 35 us -> none  [passed_along(): lax.ppermute(value, axis, [(source, source + steps) for source in range(l...]
  transfers between devices with their start and end apart: 18 -> 0, of which waited for: 12 -> 0; matrix products, arithmetic and copies ran while one was open for 4% -> 0% of each run, Pallas kernels for 0% -> 0%
where the time goes in v2:
time: 235 us
  Pallas kernels  230 us (98%)
  local copies, waits for them, and re-layouts  4.75 us (2%)
    pallas_call x1, Pallas kernels, body(): pl.pallas_call(kernel, name='reconstruct', out_shape=(jax.ShapeDtypeStruc...  230 us
    unnamed x2, local copies, waits for them, and re-layouts  4.75 us

profile of v2, /device:TPU:1, one launch (start us, length us, event | category | flops | bytes accessed | tf_op | source)
XLA Modules:
  0.0 234.9 jit_solution(13273632160972980055)
XLA Ops:
  0.6 229.5 %reconstruct.1 = (f32[2,128,256]{2,1,0:T(8,128)}, f32[2,512,512]{2,1,0:T(8,128)}) custom-call(s32[2]{0:T(128)} %cols.1, f32[2,128,256]{2,1,0:T(8,128)} %field.1, f32[2,512,512]{2,1,0:T(8,128)} %probe_in.1, f32[2,512,512]{2,1,0:T(8,128)} %amps.1, bf16[1024,1024]{1,0:T(8,128)(2,1)} %constant.4.clone.left, bf16[1024,1024]{1,0:T(8,128)(2,1)} %constant.5.clone.right), custom_call_target="tpu_custom_call" | custom-call | tf_op jit(solution)/shard_map/reconstruct/pallas_call | solution.py:481
  230.2 1.7 copy.10
  231.8 3.1 %copy.11 = f32[2,512,512]{2,1,0:T(8,128)} copy(f32[2,512,512]{2,1,0:T(8,128)} %get-tuple-element.5) | data formatting | bytes 4194304

commit v3 on v2

--- a/solution.py
+++ b/solution.py
@@ -18,7 +18,7 @@
 F32 = jnp.float32
 BF16 = jnp.bfloat16
 TILE = (2, 2, RB, 128)
-SENDS = 256
+GATHER_SENDS, REDUCE_SENDS, PROBE_SENDS = 43, 34, 53
 
 
 def tables():
@@ -40,8 +40,9 @@
 
 
 class Links:
-    def __init__(self, send_sems, recv_sems):
-        self.send_sems, self.recv_sems, self.used, self.copies = send_sems, recv_sems, 0, []
+    def __init__(self, send_sems, recv_sems, base, limit):
+        self.send_sems, self.recv_sems, self.copies = send_sems, recv_sems, []
+        self.base, self.used, self.limit = base, base, base + limit
         o, p = lax.axis_index("obj"), lax.axis_index("pat")
         self.o, self.p = o, p
         self.y, self.z, self.x, self.c = o // 4, lax.rem(o, 4), p // 2, lax.rem(p, 2)
@@ -60,11 +61,12 @@
         barrier = pltpu.get_barrier_semaphore()
         for device in near:
             pl.semaphore_signal(barrier, inc=1, device_id=device, device_id_type=MESH)
-        pl.semaphore_wait(barrier, len(near))
+        return lambda: pl.semaphore_wait(barrier, len(near))
 
     def send(self, src, dst, device):
         k = self.used
         self.used += 1
+        assert k < self.limit
         copy = pltpu.make_async_remote_copy(
             src_ref=src, dst_ref=dst, send_sem=self.send_sems.at[k], recv_sem=self.recv_sems.at[k],
             device_id=device, device_id_type=MESH,
@@ -76,7 +78,7 @@
     def drain(self):
         for copy in self.copies:
             copy.wait_send()
-        self.copies = []
+        self.copies, self.used = [], self.base
 
 
 class Gather:
@@ -103,17 +105,23 @@
             self.got["chain", b].wait_recv()
             src = self.at(b, self.me)
         dst = self.at(b, self.me)
-        self.got["up", b] = self.links.send(src, dst, self.up)
-        self.got["down", b] = self.links.send(src, dst, self.down)
+        for name, half, device in (("up", 0, self.up), ("down", 1, self.down), ("up'", 1, self.up), ("down'", 0, self.down)):
+            part = pl.ds(half, 1)
+            self.got[name, b] = self.links.send(src.at[part], dst.at[part], device)
         if 0 < b < 3:
             self.chain(b)
         self.got["sib", b] = [self.links.send(src, dst, self.sib)]
 
-    def second(self, b):
+    def relay(self, b):
         for name, pat, half, onward in (("up", self.before, 0, self.up), ("down", self.after, 1, self.down)):
             self.got[name, b].wait_recv()
-            part, whole = self.at(b, pat, half), self.at(b, pat)
+            part = self.at(b, pat, half)
             self.got[name + "2", b] = self.links.send(part, part, onward)
+
+    def second(self, b):
+        for name, pat in (("up'", self.before), ("down'", self.after)):
+            self.got[name, b].wait_recv()
+            whole = self.at(b, pat)
             self.got["sib", b].append(self.links.send(whole, whole, self.sib))
 
     def third(self, b):
@@ -134,35 +142,53 @@
         self.sib, self.up, self.down = links.target(dc=1), links.target(dx=1), links.target(dx=-1)
         x = links.x
         self.before, self.after, self.across = ring(x, -1), ring(x, 1), ring(x, 2)
+        self.pieces = (self.across, self.after, self.before, x)
         self.got = {}
 
     def zeroth(self, b):
-        self.got["sib", b] = self.links.send(self.theirs.at[b], self.sibs.at[b], self.sib)
+        for piece, spot in enumerate(self.pieces if b == 3 else (None,)):
+            at = (b,) if spot is None else (b, spot)
+            self.got["sib", b, piece] = self.links.send(self.theirs.at[at], self.sibs.at[at], self.sib)
 
     def first(self, b):
         own, sibs = self.own, self.sibs
-        self.got["sib", b].wait_recv()
-
-        @pl.loop(0, 4)
-        def _(k):
-            own[b, k] = own[b, k] + sibs[b, k]
-
-        self.got["up", b] = self.links.send(own.at[b, self.across, 0], self.halves.at[b, 0], self.up)
-        self.got["down", b] = self.links.send(own.at[b, self.across, 1], self.halves.at[b, 1], self.down)
+
+        def wait(piece):
+            if b == 3:
+                spot = self.pieces[piece]
+                self.got["sib", b, piece].wait_recv()
+                own[b, spot] = own[b, spot] + sibs[b, spot]
+
+        def go(name, pat, half, dst, device):
+            self.got[name, b] = self.links.send(own.at[b, pat, half], dst, device)
+
+        if b < 3:
+            self.got["sib", b, 0].wait_recv()
+
+            @pl.loop(0, 4)
+            def _(k):
+                own[b, k] = own[b, k] + sibs[b, k]
+
+        wait(0)
+        go("up", self.across, 0, self.halves.at[b, 0], self.up)
+        go("down", self.across, 1, self.halves.at[b, 1], self.down)
+        wait(1)
+        go("up'", self.after, 1, self.wholes.at[b, 0, 1], self.up)
+        wait(2)
+        go("down'", self.before, 0, self.wholes.at[b, 1, 0], self.down)
+        wait(3)
 
     def second(self, b):
         own = self.own
-        self.got["up", b].wait_recv()
-        own[b, self.after, 0] = own[b, self.after, 0] + self.halves[b, 0]
-        self.got["up2", b] = self.links.send(own.at[b, self.after], self.wholes.at[b, 0], self.up)
-        self.got["down", b].wait_recv()
-        own[b, self.before, 1] = own[b, self.before, 1] + self.halves[b, 1]
-        self.got["down2", b] = self.links.send(own.at[b, self.before], self.wholes.at[b, 1], self.down)
+        for name, pat, half, way, device in (("up", self.after, 0, 0, self.up), ("down", self.before, 1, 1, self.down)):
+            self.got[name, b].wait_recv()
+            own[b, pat, half] = own[b, pat, half] + self.halves[b, way]
+            self.got[name + "2", b] = self.links.send(own.at[b, pat, half], self.wholes.at[b, way, half], device)
 
     def third(self, b):
         own, x = self.own, self.links.x
-        self.got["up2", b].wait_recv()
-        self.got["down2", b].wait_recv()
+        for name in ("up'", "down'", "up2", "down2"):
+            self.got[name, b].wait_recv()
         total = own[b, x] + (self.wholes[b, 0] + self.wholes[b, 1])
         if b < 3:
             self.got["chain", b].wait_recv()
@@ -175,8 +201,9 @@
 
 class ProbeSum:
     def __init__(self, links, grad, probe, bufs, counts, counted, need_count):
+        self.axes = ("dy", "dz")
         self.links, self.grad, self.probe = links, grad, probe
-        self.from_sib, self.r1, self.s1, self.r2, self.s2, self.r3 = bufs
+        self.from_sib, self.r1, self.s1, self.r2, self.r3 = bufs
         self.counts, self.counted, self.need = counts, counted, need_count
         self.sib = links.target(dc=1)
         self.got = []
@@ -205,85 +232,106 @@
         links, grad, probe = self.links, self.grad, self.probe
         y, z, x, c = links.y, links.z, links.x, links.c
         lanes = (pl.ds(0, 256), pl.ds(256, 256))
+        outer = [(h, axis, y if axis == "dy" else z) for h, axis in enumerate(self.axes)]
+        inner = [(h, "dz" if axis == "dy" else "dy", z if axis == "dy" else y) for h, axis in enumerate(self.axes)]
+        block = [128 * place for _, _, place in outer]
+        strip = [block[h] + 32 * place for h, _, place in inner]
+
+        def piece(ref, plane, h, k):
+            _, _, place = outer[h]
+            return ref.at[plane + (rows_of(128 * ring(place, k), 128), lanes[h])]
 
         def start():
-            self.put(grad.at[1 - c], self.from_sib, dc=1)
+            for k in (2, 1, 3, 0):
+                for h in range(2):
+                    self.put(piece(grad, (1 - c,), h, k), piece(self.from_sib, (), h, k), dc=1)
             self.count_out(0, "dc")
 
         def first():
-            self.pull()
+            arriving, self.got = self.got, []
+            for n, (k, h) in enumerate((k, h) for k in (2, 1, 3, 0) for h in range(2)):
+                arriving[n].wait_recv()
+                _, axis, place = outer[h]
+                rows = rows_of(128 * ring(place, k), 128)
+                grad[c, rows, lanes[h]] = grad[c, rows, lanes[h]] + self.from_sib[rows, lanes[h]]
+                if k:
+                    self.put(piece(grad, (c,), h, k), self.r1.at[h, k - 1], **{axis: k})
+            for copy in arriving[8:]:
+                copy.wait_recv()
             self.count_in(0)
-
-            @pl.loop(0, 8)
-            def _(k):
-                rows = rows_of(k * 64, 64)
-                grad[c, rows, :] = grad[c, rows, :] + self.from_sib[rows, :]
-
-            for k in (2, 1, 3):
-                self.put(grad.at[c, rows_of(128 * ring(y, k), 128), lanes[0]], self.r1.at[0, k - 1], dy=k)
-                self.put(grad.at[c, rows_of(128 * ring(z, k), 128), lanes[1]], self.r1.at[1, k - 1], dz=k)
             self.count_out(1, "dy")
 
         def second():
             self.pull()
             self.count_in(1)
-            for h, place in ((0, y), (1, z)):
-                total = grad[c, rows_of(128 * place, 128), lanes[h]]
+            for h in range(2):
+                total = grad[c, rows_of(block[h], 128), lanes[h]]
                 self.s1[h] = total + self.r1[h, 0] + self.r1[h, 1] + self.r1[h, 2]
             for k in (2, 1, 3):
-                self.put(self.s1.at[0, rows_of(32 * ring(z, k), 32), :], self.r2.at[0, k - 1], dz=k)
-                self.put(self.s1.at[1, rows_of(32 * ring(y, k), 32), :], self.r2.at[1, k - 1], dy=k)
+                for h, axis, place in inner:
+                    self.put(self.s1.at[h, rows_of(32 * ring(place, k), 32), :], self.r2.at[h, k - 1], **{axis: k})
             self.count_out(2, "dz")
 
         def third():
             self.pull()
             self.count_in(2)
-            for h, place in ((0, z), (1, y)):
+            for h, _, place in inner:
                 total = self.s1[h, rows_of(32 * place, 32), :]
-                self.s2[h] = total + self.r2[h, 0] + self.r2[h, 1] + self.r2[h, 2]
+                self.r3[x, h] = total + self.r2[h, 0] + self.r2[h, 1] + self.r2[h, 2]
             for k in (2, 1, 3):
-                self.put(self.s2.at[:, rows_of(8 * ring(x, k), 8), :], self.r3.at[k - 1], dx=k)
+                self.put(self.r3.at[x], self.r3.at[x], dx=k)
             self.count_out(3, "dx")
 
         def fourth():
             self.pull()
             self.count_in(3)
-            total = self.s2[:, rows_of(8 * x, 8), :] + self.r3[0] + self.r3[1] + self.r3[2]
-            count = self.counts[4][:, :1]
-            for h, row in ((0, 128 * y + 32 * z + 8 * x), (1, 128 * z + 32 * y + 8 * x)):
-                spot = rows_of(row, 8)
-                probe[c, spot, lanes[h]] = probe[c, spot, lanes[h]] + total[h] / count
+            count = self.counts[4][:1, :1]
+            for h, axis, _ in inner:
+                total = self.r3[0, h] + self.r3[1, h] + self.r3[2, h] + self.r3[3, h]
+                rows = rows_of(strip[h], 32)
+                probe[c, rows, lanes[h]] = probe[c, rows, lanes[h]] + total / count
+                spot = probe.at[c, rows, lanes[h]]
                 for k in (2, 1, 3):
-                    self.put(probe.at[c, spot, lanes[h]], probe.at[c, spot, lanes[h]], dx=k)
+                    self.put(spot, spot, **{axis: k})
 
         def fifth():
             self.pull()
-            for h, row, axis in ((0, 128 * y + 32 * z, "dz"), (1, 128 * z + 32 * y, "dy")):
-                spot = probe.at[c, rows_of(row, 32), lanes[h]]
-                for k in (2, 1, 3):
-                    self.put(spot, spot, **{axis: k})
+            for k in (2, 1, 3):
+                for h, axis, _ in outer:
+                    self.put(piece(probe, (c,), h, 0), piece(probe, (c,), h, 0), **{axis: k})
+            self.home = []
+            self.onward(0)
 
         def sixth():
-            self.pull()
-            for h, row, axis in ((0, 128 * y, "dy"), (1, 128 * z, "dz")):
-                spot = probe.at[c, rows_of(row, 128), lanes[h]]
-                for k in (2, 1, 3):
-                    self.put(spot, spot, **{axis: k})
+            arriving, self.got = self.got, []
+            for n, k in enumerate((2, 1, 3)):
+                for h in range(2):
+                    arriving[2 * n + h].wait_recv()
+                    self.onward(-k, (h,))
+
+        def onward(k, parts=(0, 1)):
+            for h in parts:
+                spot = piece(probe, (c,), h, k)
+                self.home.append(self.links.send(spot, spot, self.sib))
 
         def seventh():
-            self.pull()
-            self.put(probe.at[c], probe.at[c], dc=1)
-
-        return [start, first, second, third, fourth, fifth, sixth, seventh, self.pull]
+            for copy in self.home:
+                copy.wait_recv()
+
+        self.onward = onward
+        return [start, first, second, third, fourth, fifth, sixth, seventh]
 
 
 def kernel(cols, field, probe_in, amps, left, right, field_out, probe_out,
            band0, band1, band2, band3, tile, probe, amp, lt, rt, patch, flat, tall, wave, back, parts0, parts1,
            probe_grad, own, theirs, sibs, halves, wholes, chained,
-           from_sib, r1, s1, r2, s2, r3, counts, counted, send_sems, recv_sems, sems):
+           from_sib, r1, s1, r2, r3, counts, counted, send_sems, recv_sems, sems):
     bands = (band0, band1, band2, band3)
     parts = (parts0, parts1)
-    links = Links(send_sems, recv_sems)
+    links = Links(send_sems, recv_sems, 0, GATHER_SENDS)
+    sum_links = Links(send_sems, recv_sems, GATHER_SENDS, REDUCE_SENDS)
+    probe_links = Links(send_sems, recv_sems, GATHER_SENDS + REDUCE_SENDS, PROBE_SENDS)
+    met = links.greet()
     loads = [
         pltpu.make_async_copy(src, dst, sems.at[i])
         for i, (src, dst) in enumerate(((probe_in, probe), (left, lt), (right, rt), (amps, amp)))
@@ -301,7 +349,7 @@
     valid = [(cols[s] >= 0).astype(F32) for s in range(SLOTS)]
     counts[0] = jnp.full((8, 128), valid[0] + valid[1], F32)
     lane = lax.broadcasted_iota(jnp.int32, (32, 128), 1)
-    links.greet()
+    met()
 
     def product(lhs, rhs):
         return jnp.dot(lhs, rhs, preferred_element_type=F32)
@@ -396,89 +444,109 @@
         gather.first(0)
         own_copy = pltpu.make_async_copy(tile, gather.at(0, gather.me), sems.at[4])
         own_copy.start()
+        gather.relay(0)
+        gather.first(1)
         gather.second(0)
-        gather.first(1)
+        if turn:
+            p[6]()
         gather.third(0)
+        gather.relay(1)
         if turn == 0:
             for load in loads:
                 load.wait()
-        else:
-            tail[0]()
+        gather.first(2)
+        gather.second(1)
         own_copy.wait()
-        gather.second(1)
-        gather.first(2)
+        gather.third(1)
+        gather.relay(2)
+        gather.first(3)
         if turn:
-            tail[1]()
+            p[7]()
         gather.done(0)
         rows_in(0)
-        gather.third(1)
         gather.second(2)
-        gather.first(3)
         gather.done(1)
         rows_in(1)
         gather.third(2)
-        gather.second(3)
+        gather.relay(3)
         gather.done(2)
         rows_in(2)
+        gather.second(3)
         gather.third(3)
         gather.done(3)
         rows_in(3)
         links.drain()
         middle()
-        reduce = Reduce(links, own, theirs, sibs, halves, wholes, chained)
-        sums = ProbeSum(links, probe_grad, probe, (from_sib, r1, s1, r2, s2, r3), counts, counted, turn == 0).steps()
+        if turn:
+            sum_links.drain()
+            probe_links.drain()
+        r = Reduce(sum_links, own, theirs, sibs, halves, wholes, chained)
+        sums = ProbeSum(probe_links, probe_grad, probe, (from_sib, r1, s1, r2, r3), counts, counted, turn == 0)
+        p = sums.steps()
         rows_out(3)
-        reduce.zeroth(3)
+        r.zeroth(3)
         rows_out(2)
-        reduce.zeroth(2)
-        reduce.first(3)
+        r.zeroth(2)
+        r.first(3)
         rows_out(1)
-        reduce.zeroth(1)
-        reduce.first(2)
-        reduce.second(3)
+        r.zeroth(1)
+        r.second(3)
+        r.first(2)
         rows_out(0)
-        reduce.zeroth(0)
-        sums[0]()
-        reduce.first(1)
-        sums[1]()
-        reduce.second(2)
-        reduce.third(3)
-        reduce.first(0)
-        sums[2]()
-        reduce.second(1)
-        sums[3]()
-        reduce.third(2)
-        sums[4]()
-        reduce.second(0)
-        sums[5]()
-        reduce.third(1)
-        sums[6]()
-        total = reduce.third(0)
-        tail = sums[7:]
-        if turn < ITERS - 1:
-            tile[...] = tile[...] + 0.25 * total
+        p[0]()
+        r.zeroth(0)
+        if turn == 0:
+            order = ((r.third, 3), p[1], (r.second, 2), (r.first, 1), (r.third, 2), (r.second, 1), p[2], (r.first, 0),
+                     p[3], (r.third, 1), (r.second, 0), p[4], p[5], (r.third, 0))
+        else:
+            order = (p[1], (r.third, 3), (r.second, 2), (r.first, 1), p[2], (r.third, 2), p[3], (r.second, 1),
+                     (r.first, 0), p[4], (r.third, 1), (r.second, 0), p[5], (r.third, 0), p[6])
+        for step in order:
+            if isinstance(step, tuple):
+                total = step[0](step[1])
+                if step == (r.third, 0):
+                    tile[...] = tile[...] + 0.25 * total
+            else:
+                step()
     for t in range(2):
-        field_out[:, :, 128 * t:128 * t + 128] = tile[t] + 0.25 * total[t]
-    tail[0]()
+        field_out[:, :, 128 * t:128 * t + 128] = tile[t]
     mine = pltpu.make_async_copy(probe.at[links.c], probe_out.at[links.c], sems.at[5])
     mine.start()
-    tail[1]()
+    p[7]()
     other = pltpu.make_async_copy(probe.at[1 - links.c], probe_out.at[1 - links.c], sems.at[6])
     other.start()
-    links.drain()
+    sum_links.drain()
+    probe_links.drain()
     mine.wait()
     other.wait()
 
 
+def hand_out(field, probe, field_out, probe_out, field_held, probe_held, sems):
+    ways = [(field, field_held, field_out)]
+    for k in range(8):
+        part = (k // 4, pl.ds(128 * (k % 4), 128))
+        ways.append((probe.at[part], probe_held.at[part], probe_out.at[part]))
+    ins = [pltpu.make_async_copy(src, held, sems.at[0, k]) for k, (src, held, _) in enumerate(ways)]
+    outs = [pltpu.make_async_copy(held, dst, sems.at[1, k]) for k, (_, held, dst) in enumerate(ways)]
+    for copy in ins:
+        copy.start()
+    for arrived, onward in zip(ins, outs):
+        arrived.wait()
+        onward.start()
+    for copy in outs:
+        copy.wait()
+
+
 def f32(*shape):
     return pltpu.VMEM(shape, F32)
 
 
 def body(object_field, probe, scan_cols, amplitudes):
     left, right = (jnp.asarray(t) for t in tables())
+    sends = GATHER_SENDS + REDUCE_SENDS + PROBE_SENDS
     anywhere = pl.BlockSpec(memory_space=pl.ANY)
     vmem = pl.BlockSpec(memory_space=pltpu.VMEM)
-    return pl.pallas_call(
+    field, probe = pl.pallas_call(
         kernel,
         name="reconstruct",
         out_shape=(jax.ShapeDtypeStruct((2, RB, 256), F32), jax.ShapeDtypeStruct((2, N, N), F32)),
@@ -490,12 +558,21 @@
             f32(1024, 256), f32(RB, 1024), f32(7, 2, RB, 128), f32(7, 2, RB, 128),
             f32(2, N, N), f32(4, 4, *TILE), f32(4, 4, *TILE), f32(4, 4, *TILE),
             f32(4, 2, 2, RB, 128), f32(4, 2, *TILE), f32(3, *TILE),
-            f32(N, N), f32(2, 3, 128, 256), f32(2, 128, 256), f32(2, 3, 32, 256), f32(2, 32, 256), f32(3, 2, 8, 256),
+            f32(N, N), f32(2, 3, 128, 256), f32(2, 128, 256), f32(2, 3, 32, 256), f32(4, 2, 32, 256),
             f32(5, 8, 128), f32(4, 3, 8, 128),
-            pltpu.SemaphoreType.DMA((SENDS,)), pltpu.SemaphoreType.DMA((SENDS,)), pltpu.SemaphoreType.DMA((7,)),
+            pltpu.SemaphoreType.DMA((sends,)), pltpu.SemaphoreType.DMA((sends,)), pltpu.SemaphoreType.DMA((7,)),
         ],
         compiler_params=pltpu.CompilerParams(vmem_limit_bytes=60 << 20, collective_id=1, has_side_effects=True),
     )(scan_cols, object_field, probe, amplitudes, left, right)
+    return pl.pallas_call(
+        hand_out,
+        name="hand_out",
+        out_shape=(jax.ShapeDtypeStruct((2, RB, 256), F32), jax.ShapeDtypeStruct((2, N, N), F32)),
+        in_specs=[anywhere] * 2,
+        out_specs=(anywhere, anywhere),
+        scratch_shapes=[f32(2, RB, 256), f32(2, N, N), pltpu.SemaphoreType.DMA((2, 9))],
+        compiler_params=pltpu.CompilerParams(vmem_limit_bytes=16 << 20),
+    )(field, probe)
 
 
 def solution(mesh):

time: 235 us -> 227 us (0.966)
  Pallas kernels: 230 us -> 222 us
    pallas_call x1, Pallas kernels: 230 us -> 220 us  [body(): pl.pallas_call(kernel, name='reconstruct', out_shape=(jax.ShapeDtypeStruc...]
    unnamed x2 -> x4, local copies, waits for them, and re-layouts: 4.75 us -> 2.53 us
where the time goes in v3:
time: 227 us; the launch traced here: 225 us
  Pallas kernels  222 us (98%)
  local copies, waits for them, and re-layouts  2.53 us (1%)
    pallas_call x1, Pallas kernels, body(): pl.pallas_call(kernel, name='reconstruct', out_shape=(jax.ShapeDtypeStruc...  220 us

profile of v3, /device:TPU:1, one launch (start us, length us, event | category | flops | bytes accessed | tf_op | source)
XLA Modules:
  0.0 225.5 jit_solution(15951280959930819315)
XLA Ops:
  0.6 220.4 %reconstruct.1 = (f32[2,128,256]{2,1,0:T(8,128)}, f32[2,512,512]{2,1,0:T(8,128)}) custom-call(s32[2]{0:T(128)} %cols.1, f32[2,128,256]{2,1,0:T(8,128)} %field.1, f32[2,512,512]{2,1,0:T(8,128)} %probe_in.1, f32[2,512,512]{2,1,0:T(8,128)} %amps.1, bf16[1024,1024]{1,0:T(8,128)(2,1)} %constant.4.clone.left, bf16[1024,1024]{1,0:T(8,128)(2,1)} %constant.5.clone.right), custom_call_target="tpu_custom_call" | custom-call | tf_op jit(solution)/shard_map/reconstruct/pallas_call | solution.py:549
  221.0 0.0 copy-start
  221.1 1.6 copy-done
  222.6 0.0 copy-start.1
  222.6 0.9 copy-done.1
  223.6 1.7 hand_out.1
Async XLA Ops:
  221.0 1.6 copy-start
  222.6 0.9 copy-start.1

commit v4 on v3

--- a/solution.py
+++ b/solution.py
@@ -36,6 +36,8 @@
 
 
 def rows_of(start, count):
+    if isinstance(start, int):
+        return pl.ds(start, count)
     return pl.ds(pl.multiple_of(start, count), count)
 
 
@@ -357,8 +359,7 @@
     def rows_in(b):
         inside = links.o + b < GROUPS
         for s in range(SLOTS):
-            @pl.loop(0, 4)
-            def _(m):
+            for m in range(4):
                 rows = rows_of(m * 32, 32)
                 whole = rows_of(b * RB + m * 32, 32)
                 loaded = [[bands[b][jnp.minimum(base[s] + j, 15), part, rows, :] for j in range(5)] for part in (0, 1)]
@@ -382,29 +383,39 @@
             tall[s, N + b * RB:N + b * RB + RB, :] = mid[:, N:]
 
     def middle():
-        for s in range(SLOTS):
-            for n in range(2):
-                cut = slice(256 * n, 256 * n + 256)
-                wave[...] = product(lt[...], tall[s, :, cut])
-
-                @pl.loop(0, 16)
-                def _(m):
-                    upper, lower = rows_of(m * 32, 32), rows_of(N + m * 32, 32)
-                    re, im = wave[upper, :], wave[lower, :]
-                    factor = amp[s, upper, cut] * lax.rsqrt(jnp.maximum(re * re + im * im, 0.0625))
-                    tall[s, upper, cut] = (re * factor).astype(BF16)
-                    tall[s, lower, cut] = (im * factor).astype(BF16)
-
-                mid = product(rt[...], tall[s, :, cut]).astype(BF16)
-                flat[s, :, cut] = mid[:N]
-                flat[s, :, 512 + 256 * n:768 + 256 * n] = mid[N:]
+        blocks = [(s, slice(256 * n, 256 * n + 256)) for s in range(SLOTS) for n in range(2)]
+
+        def spread(i, r):
+            s, cut = blocks[i]
+            for start in (128 * r, N + 128 * r):
+                wave[i % 2, start:start + 128, :] = product(lt[start:start + 128, :], tall[s, :, cut])
+
+        def limit(i, r):
+            s, cut = blocks[i]
+            for m in range(128 * r, 128 * r + 128, 32):
+                upper, lower = slice(m, m + 32), slice(N + m, N + m + 32)
+                re, im = wave[i % 2, upper, :], wave[i % 2, lower, :]
+                factor = amp[s, upper, cut] * lax.rsqrt(jnp.maximum(re * re + im * im, 0.0625))
+                tall[s, upper, cut] = (re * factor).astype(BF16)
+                tall[s, lower, cut] = (im * factor).astype(BF16)
+
+        for r in range(4):
+            spread(0, r)
+        for i, (s, cut) in enumerate(blocks):
+            for r in range(4):
+                if i + 1 < len(blocks):
+                    spread(i + 1, r)
+                limit(i, r)
+            for start in range(0, N, 256):
+                rows = slice(start, start + 256)
+                flat[s, rows, cut] = product(rt[rows, :], tall[s, :, cut]).astype(BF16)
+                flat[s, rows, N + cut.start:N + cut.stop] = product(rt[N + start:N + start + 256, :], tall[s, :, cut]).astype(BF16)
 
     def rows_out(b):
         for s in range(SLOTS):
             back[...] = product(flat[s, b * RB:b * RB + RB, :], lt[...])
 
-            @pl.loop(0, 4)
-            def _(m):
+            for m in range(4):
                 rows = rows_of(m * 32, 32)
                 whole = rows_of(b * RB + m * 32, 32)
                 last = [jnp.zeros((32, 128), F32)] * 2
@@ -555,7 +566,7 @@
         scratch_shapes=[f32(16, 2, RB, 128)] * 4 + [
             f32(*TILE), f32(2, N, N), f32(2, N, N), pltpu.VMEM((1024, 1024), BF16), pltpu.VMEM((1024, 1024), BF16),
             f32(2, 2, N, N), pltpu.VMEM((2, N, 1024), BF16), pltpu.VMEM((2, 1024, N), BF16),
-            f32(1024, 256), f32(RB, 1024), f32(7, 2, RB, 128), f32(7, 2, RB, 128),
+            f32(2, 1024, 256), f32(RB, 1024), f32(7, 2, RB, 128), f32(7, 2, RB, 128),
             f32(2, N, N), f32(4, 4, *TILE), f32(4, 4, *TILE), f32(4, 4, *TILE),
             f32(4, 2, 2, RB, 128), f32(4, 2, *TILE), f32(3, *TILE),
             f32(N, N), f32(2, 3, 128, 256), f32(2, 128, 256), f32(2, 3, 32, 256), f32(4, 2, 32, 256),

time: 227 us -> 207 us (0.912)
  Pallas kernels: 222 us -> 203 us
    pallas_call x1, Pallas kernels: 220 us -> 201 us  [body(): pl.pallas_call(kernel, name='reconstruct', out_shape=(jax.ShapeDtypeStruc...]
where the time goes in v4:
time: 207 us; the launch traced here: 206 us
  Pallas kernels  203 us (98%)
  local copies, waits for them, and re-layouts  2.53 us (1%)
    pallas_call x1, Pallas kernels, body(): pl.pallas_call(kernel, name='reconstruct', out_shape=(jax.ShapeDtypeStruc...  201 us

profile of v4, /device:TPU:1, one launch (start us, length us, event | category | flops | bytes accessed | tf_op | source)
XLA Modules:
  0.0 206.3 jit_solution(8556198013540388732)
XLA Ops:
  0.6 201.2 %reconstruct.1 = (f32[2,128,256]{2,1,0:T(8,128)}, f32[2,512,512]{2,1,0:T(8,128)}) custom-call(s32[2]{0:T(128)} %cols.1, f32[2,128,256]{2,1,0:T(8,128)} %field.1, f32[2,512,512]{2,1,0:T(8,128)} %probe_in.1, f32[2,512,512]{2,1,0:T(8,128)} %amps.1, bf16[1024,1024]{1,0:T(8,128)(2,1)} %constant.4.clone.left, bf16[1024,1024]{1,0:T(8,128)(2,1)} %constant.5.clone.right), custom_call_target="tpu_custom_call" | custom-call | tf_op jit(solution)/shard_map/reconstruct/pallas_call | solution.py:560
  201.9 0.0 copy-start
  201.9 1.6 copy-done
  203.5 0.0 copy-start.1
  203.5 0.9 copy-done.1
  204.4 1.7 hand_out.1
Async XLA Ops:
  201.9 1.6 copy-start
  203.5 0.9 copy-start.1

commit v5 on v4

--- a/solution.py
+++ b/solution.py
@@ -457,9 +457,9 @@
         own_copy.start()
         gather.relay(0)
         gather.first(1)
+        if turn:
+            p[5]()
         gather.second(0)
-        if turn:
-            p[6]()
         gather.third(0)
         gather.relay(1)
         if turn == 0:
@@ -472,6 +472,7 @@
         gather.relay(2)
         gather.first(3)
         if turn:
+            p[6]()
             p[7]()
         gather.done(0)
         rows_in(0)
@@ -500,15 +501,15 @@
         r.zeroth(2)
         r.first(3)
         rows_out(1)
+        rows_out(0)
+        p[0]()
         r.zeroth(1)
+        r.zeroth(0)
         r.second(3)
         r.first(2)
-        rows_out(0)
-        p[0]()
-        r.zeroth(0)
         if turn == 0:
             order = ((r.third, 3), p[1], (r.second, 2), (r.first, 1), (r.third, 2), (r.second, 1), p[2], (r.first, 0),
-                     p[3], (r.third, 1), (r.second, 0), p[4], p[5], (r.third, 0))
+                     p[3], (r.third, 1), (r.second, 0), p[4], (r.third, 0))
         else:
             order = (p[1], (r.third, 3), (r.second, 2), (r.first, 1), p[2], (r.third, 2), p[3], (r.second, 1),
                      (r.first, 0), p[4], (r.third, 1), (r.second, 0), p[5], (r.third, 0), p[6])

time: 207 us -> 205 us (level)
  no operation moved by 1% of the time
where the time goes in v5:
time: 205 us; the launch traced here: 204 us
  Pallas kernels  201 us (98%)
  local copies, waits for them, and re-layouts  2.53 us (1%)
    pallas_call x1, Pallas kernels, body(): pl.pallas_call(kernel, name='reconstruct', out_shape=(jax.ShapeDtypeStruc...  199 us

profile of v5, /device:TPU:1, one launch (start us, length us, event | category | flops | bytes accessed | tf_op | source)
XLA Modules:
  0.0 204.3 jit_solution(2461172412721706991)
XLA Ops:
  0.6 199.3 %reconstruct.1 = (f32[2,128,256]{2,1,0:T(8,128)}, f32[2,512,512]{2,1,0:T(8,128)}) custom-call(s32[2]{0:T(128)} %cols.1, f32[2,128,256]{2,1,0:T(8,128)} %field.1, f32[2,512,512]{2,1,0:T(8,128)} %probe_in.1, f32[2,512,512]{2,1,0:T(8,128)} %amps.1, bf16[1024,1024]{1,0:T(8,128)(2,1)} %constant.4.clone.left, bf16[1024,1024]{1,0:T(8,128)(2,1)} %constant.5.clone.right), custom_call_target="tpu_custom_call" | custom-call | tf_op jit(solution)/shard_map/reconstruct/pallas_call | solution.py:561
  199.9 0.0 copy-start
  199.9 1.6 copy-done
  201.5 0.0 copy-start.1
  201.5 0.9 copy-done.1
  202.4 1.7 hand_out.1
Async XLA Ops:
  199.9 1.6 copy-start
  201.5 0.9 copy-start.1

commit v6 on v5

--- a/solution.py
+++ b/solution.py
@@ -470,9 +470,10 @@
         own_copy.wait()
         gather.third(1)
         gather.relay(2)
+        if turn:
+            p[6]()
         gather.first(3)
         if turn:
-            p[6]()
             p[7]()
         gather.done(0)
         rows_in(0)

time: 205 us -> 205 us (level)
  no operation moved by 1% of the time
where the time goes in v6:
time: 205 us
  Pallas kernels  202 us (99%)
  local copies, waits for them, and re-layouts  2.53 us (1%)
    pallas_call x1, Pallas kernels, body(): pl.pallas_call(kernel, name='reconstruct', out_shape=(jax.ShapeDtypeStruc...  200 us

profile of v6, /device:TPU:1, one launch (start us, length us, event | category | flops | bytes accessed | tf_op | source)
XLA Modules:
  0.0 205.2 jit_solution(7263588798161807482)
XLA Ops:
  0.6 200.1 %reconstruct.1 = (f32[2,128,256]{2,1,0:T(8,128)}, f32[2,512,512]{2,1,0:T(8,128)}) custom-call(s32[2]{0:T(128)} %cols.1, f32[2,128,256]{2,1,0:T(8,128)} %field.1, f32[2,512,512]{2,1,0:T(8,128)} %probe_in.1, f32[2,512,512]{2,1,0:T(8,128)} %amps.1, bf16[1024,1024]{1,0:T(8,128)(2,1)} %constant.4.clone.left, bf16[1024,1024]{1,0:T(8,128)(2,1)} %constant.5.clone.right), custom_call_target="tpu_custom_call" | custom-call | tf_op jit(solution)/shard_map/reconstruct/pallas_call | solution.py:562
  200.7 0.0 copy-start
  200.8 1.6 copy-done
  202.3 0.0 copy-start.1
  202.3 0.9 copy-done.1
  203.3 1.7 hand_out.1
Async XLA Ops:
  200.7 1.6 copy-start
  202.3 0.9 copy-start.1
